TPU v7x, 256 devices: a whole 4x4x8 slice. The times are simulated.
256 devices in a mesh: expert: 16 (over z_lo, x), dp: 16 (over y, z_hi, core).
Axes of the slice: x: 4, y: 4, z: 8 (z_hi: 2, z_lo: 4; z = z_hi * 4 + z_lo), core: 2. Of those that a mesh axis runs over, the one named last changes fastest.
Arguments:
- queries: bfloat16 [32768, 18432], P(('expert', 'dp')), may hold values from -32 to 32
- new_latent: bfloat16 [32768, 576], P(('expert', 'dp')), may hold values from -4 to 4
- held_pages: bfloat16 [16, 128, 36864], P('expert', 'dp'), may hold values from -4 to 4
- page_list: int32 [256, 16], P(('expert', 'dp')), may hold values from 0 to 127, as said below
- token_expert: int32 [32768, 1], P(('expert', 'dp')), may hold values from 0 to 383, as said below
- gate: float32 [32768, 1], P(('expert', 'dp')), may hold values from 0.3 to 3
- expert_rows: bfloat16 [16, 16, 16, 9, 7168], P('expert', 'dp'), may hold values from -6 to 6
- page_table: int32 [16, 32], P('expert', 'dp'), may hold values from 0 to 31, each once within a row
Outputs:
- context: bfloat16 [32768, 16384], P(('expert', 'dp'))
- moe_out: bfloat16 [32768, 7168], P(('expert', 'dp'))
- decode_pool: bfloat16 [16, 32, 36864], P('expert', 'dp')
Inputs may be any that keep to these rules, and one draw needn't show every extreme that they name: `page_list`: each span lists 16 distinct pages of its pool, at most 2 from the 8 pages of one holder (holder = page // 8), and exactly 2 from at least one holder. `token_expert`: for every span, at most 9 of its (token, slot) pairs name experts of one expert index (expert // 24), and exactly 9 for some index. `page_table`: each row is a permutation.
All inputs are finite; a program needn't handle non-finite values.
Results may differ from a plain program's by a relative error of at most 0.012.
Values may be sent and summed in bfloat16 or wider, within the bound.
No kernel may reach another device: no remote copies, remote signals or barrier semaphores. Data moves between devices by JAX's collectives and lax.ppermute only.
A program may use at most 128 MiB of HBM per device.

v0:
```python
import jax
import jax.numpy as jnp
from jax import lax
from jax.sharding import PartitionSpec as P

EXP_GROUP = 24
LAT = 512


score_scale = 0.07216878364870322


def attend(queries, key_rows):
    tokens_here = queries.shape[0]
    key_width = key_rows.shape[1]
    head_count = queries.shape[1] // key_width
    query_heads = queries.reshape(tokens_here, head_count, key_width)
    scores = (
        jnp.einsum("thc,kc->htk", query_heads, key_rows, preferred_element_type=jnp.float32)
        * score_scale
    )
    prefix = key_rows.shape[0] - tokens_here
    allowed = jnp.arange(key_rows.shape[0])[None, :] - prefix <= jnp.arange(tokens_here)[:, None]
    scores = jnp.where(allowed[None], scores, -jnp.inf)
    largest = jnp.max(scores, axis=2, keepdims=True)
    weights = jnp.exp(scores - largest)
    probabilities = (weights / jnp.sum(weights, axis=2, keepdims=True)).astype(jnp.bfloat16)
    context = jnp.einsum(
        "htk,kc->thc", probabilities, key_rows[:, :LAT], preferred_element_type=jnp.float32
    )
    return context.astype(jnp.bfloat16).reshape(tokens_here, head_count * LAT)


def combine(token_expert, gate, expert_rows):
    group_count = lax.axis_size("expert")
    capacity = expert_rows.shape[3]
    width = expert_rows.shape[4]
    blocks = expert_rows.reshape(group_count, capacity, width)
    arrived = lax.all_to_all(blocks, "expert", split_axis=0, concat_axis=0, tiled=True)
    groups = (token_expert // EXP_GROUP).reshape(-1)
    onehot = (groups[:, None] == jnp.arange(group_count, dtype=jnp.int32)[None, :]).astype(
        jnp.int32
    )
    ranking = jnp.sum((jnp.cumsum(onehot, axis=0) - onehot) * onehot, axis=1)
    slot_ids = groups * capacity + ranking
    picker = (
        slot_ids[:, None] == jnp.arange(group_count * capacity, dtype=jnp.int32)[None, :]
    ).astype(jnp.bfloat16)
    picked = jnp.dot(
        picker, arrived.reshape(group_count * capacity, width), preferred_element_type=jnp.float32
    )
    weighted = picked.reshape(gate.shape[0], gate.shape[1], width) * gate[:, :, None]
    return jnp.sum(weighted, axis=1).astype(jnp.bfloat16)


def shards(queries, new_latent, held_pages, page_list, token_expert, gate, expert_rows, page_table):
    listed = page_list.reshape(-1)
    page_width = held_pages.shape[2]
    portion = lax.all_gather(held_pages, "dp", axis=1, tiled=True)
    piece_rows = portion.shape[1]
    shifted = listed[:, None]
    picker = (shifted == jnp.arange(piece_rows, dtype=jnp.int32)[None, :]).astype(jnp.bfloat16)
    fetched = jnp.dot(picker, portion[0], preferred_element_type=jnp.float32).astype(jnp.bfloat16)
    entry_width = new_latent.shape[1]
    key_rows = jnp.concatenate([fetched.reshape(-1, entry_width), new_latent], axis=0)
    context = attend(queries, key_rows)
    moe_out = combine(token_expert, gate, expert_rows)
    new_count = page_table.shape[1]
    own_row = lax.axis_index("dp")
    new_pages = new_latent.reshape(new_count, page_width)
    targets = page_table.reshape(new_count)
    portion_pages = lax.all_gather(new_pages, "dp", axis=0, tiled=True)
    portion_targets = lax.all_gather(targets, "dp", axis=0, tiled=True)
    wanted = own_row * new_count + jnp.arange(new_count, dtype=jnp.int32)
    picker = (wanted[:, None] == portion_targets[None, :]).astype(jnp.bfloat16)
    decode_slots = jnp.dot(picker, portion_pages, preferred_element_type=jnp.float32)
    decode_pool = decode_slots.astype(jnp.bfloat16).reshape(1, new_count, page_width)
    return (context, moe_out, decode_pool)


def solution(mesh):
    return jax.shard_map(
        shards,
        mesh=mesh,
        in_specs=(
            P(("expert", "dp"), None),
            P(("expert", "dp"), None),
            P("expert", "dp", None),
            P(("expert", "dp"), None),
            P(("expert", "dp"), None),
            P(("expert", "dp"), None),
            P("expert", "dp", None, None, None),
            P("expert", "dp"),
        ),
        out_specs=(P(("expert", "dp"), None), P(("expert", "dp"), None), P("expert", "dp", None)),
        check_vma=False,
    )
```

profile of v0, /device:TPU:1, one launch (start us, length us, event | category | flops | bytes accessed | tf_op | source)
XLA Modules:
  0.0 277.6 jit_solution(8580214070443458644)
XLA Ops:
  7.2 0.0 all-gather.7.cloned.1.call-start
  7.2 1.1 copy.25
  8.3 0.9 reshape.84
  9.2 0.0 all-gather.7.cloned.1.call-update
  9.2 0.0 all-gather.5.cloned.1.call-start
  9.2 0.7 all-gather.5.cloned.1.call-update
  9.9 4.8 %copy.29 = bf16[1,1,16,9,7168]{4,3,2,1,0:T(8,128)(2,1)} copy(bf16[1,1,16,9,7168]{4,2,3,1,0:T(8,128)(2,1)} %param.14) | data formatting | bytes 4128768 | tf_op args[6]
  14.7 9.1 %all-to-all-start = ((bf16[16,9,7168]{2,1,0:T(8,128)(2,1)}), bf16[16,9,7168]{2,1,0:T(8,128)(2,1)}, u32[]{:S(2)}, u32[]{:S(2)}) async-start(bf16[16,9,7168]{2,1,0:T(8,128)(2,1)} %bitcast.45), calls=%async_computation | async-start | bytes 7340032 | tf_op jit(solution)/shard_map/all_to_all | solution.py:39
  23.8 0.0 copy-start.4
  23.8 0.0 copy-start.5
  23.8 0.0 copy-start.3
  23.8 6.7 %copy.22 = bf16[128,18432]{0,1:T(8,128)(2,1)} copy(bf16[128,18432]{1,0:T(8,128)(2,1)} %param.8) | data formatting | bytes 9437184 | tf_op args[0]
  30.5 0.1 fusion.17
  30.6 0.2 reduce_window_sum.11
  30.8 0.6 dynamic-slice
  32.0 0.1 bitcast_dynamic-update-slice_fusion
  32.1 77.9 %all-reduce = s32[32]{0:T(128)S(1)} all-reduce(s32[32]{0:T(128)S(1)} %bitcast_dynamic-update-slice_fusion), channel_id=2, replica_groups=mesh['expert'=16,'dp'=16] {'dp'}, use_global_device_ids=true, to_apply=%add | all-reduce | flops 32 | bytes 256
  110.0 0.2 select_reduce_fusion
  110.2 0.2 iota_compare_fusion
  110.5 0.0 all-to-all-done
  110.5 2.8 %reshape.76 = bf16[144,7168]{1,0:T(8,128)(2,1)S(1)} reshape(bf16[16,9,7168]{2,1,0:T(8,128)(2,1)} %all-to-all-done) | data formatting | bytes 4128768 | tf_op jit(solution)/shard_map/reshape | solution.py:50
  113.3 1.9 fusion.8
  115.2 2.9 %reshape.85 = bf16[32,36864]{1,0:T(8,128)(2,1)S(1)} reshape(bf16[16,2,36864]{2,1,0:T(2,128)(2,1)} %all-gather.7.cloned.1.call-done) | data formatting | bytes 4718592
  118.1 1.2 fusion.1
  119.2 101.9 %all-gather.5.cloned.1.call-done = bf16[1,128,36864]{2,1,0:T(8,128)(2,1)} async-done(((bf16[1,8,36864]{2,1,0:T(8,128)(2,1)}), bf16[1,128,36864]{2,1,0:T(8,128)(2,1)}) %all-gather.5.cloned.1.call-update) | async-done | bytes 9437200 | tf_op jit(solution)/shard_map/all_gather | solution.py:59
  221.1 5.1 %convolution_convert_fusion = bf16[16,36864]{1,0:T(8,128)(2,1)S(1)} fusion(bf16[1,128,36864]{2,1,0:T(8,128)(2,1)} %all-gather.5.cloned.1.call-done, s32[16]{0:T(128)S(1)} %bitcast.49), kind=kOutput, calls=%fused_computation.1 | convolution fusion | flops 151586816 | bytes 10616896 | tf_op jit(solution)/shard_map/dot_general | solution.py:63
  226.2 1.6 reshape.72
  227.8 0.6 copy.21
  228.5 13.0 %convolution_multiply_fusion = f32[1152,128,32]{1,0,2:T(8,128)} fusion(bf16[128,32,576]{0,2,1:T(8,128)(2,1)} %bitcast.46, bf16[128,576]{0,1:T(8,128)(2,1)S(1)} %copy-done, bf16[1024,576]{0,1:T(8,128)(2,1)S(1)} %copy.21), kind=kOutput, calls=%fused_computation.5 | convolution fusion | flops 5443190784 | bytes 24920064 | tf_op jit(solution)/shard_map/thc,kc->htk/dot_general | solution.py:19
  241.5 10.6 %exponential_reduce_fusion = f32[32,128]{1,0:T(8,128)S(1)} fusion(f32[1152,128,32]{1,0,2:T(8,128)} %convolution_multiply_fusion, pred[128,1152]{0,1:T(8,128)(4,1)S(1)} %iota_compare_fusion), kind=kOutput, calls=%fused_computation.9 | output fusion | flops 14156927 | bytes 19038208 | tf_op jit(solution)/shard_map/sub | solution.py:26
  252.1 12.3 %fusion.9 = bf16[512,32,128]{2,0,1:T(8,128)(2,1)} fusion(f32[32,128]{1,0:T(8,128)S(1)} %exponential_reduce_fusion, bf16[1024,576]{0,1:T(8,128)(2,1)S(1)} %copy.21, bf16[128,576]{0,1:T(8,128)(2,1)S(1)} %copy-done, f32[1152,128,32]{1,0,2:T(8,128)} %convolution_multiply_fusion, pred[128,1152]{0,1:T(8,128)(4,1)S(1)} %iota_compare_fusion), kind=kOutput, calls=%fused_computation.17 | convolution fusion | flops 4855174144 | bytes 24559616 | tf_op jit(solution)/shard_map/htk,kc->thc/dot_general | solution.py:28
  264.4 6.4 %copy.26 = bf16[128,16384]{1,0:T(8,128)(2,1)} copy(bf16[128,16384]{0,1:T(8,128)(2,1)} %bitcast.47) | data formatting | bytes 8388608
  (15 shorter events, 0.1 us)
Async XLA Ops:
  7.2 108.0 %all-gather.7.cloned.1.call-start = ((), (), s32[]{:S(2)}) async-start(), calls=%async_computation.2 | async-start | bytes 2506752 | tf_op jit(solution)/shard_map/all_gather | solution.py:72
  9.2 211.9 %all-gather.5.cloned.1.call-start = ((), (), s32[]{:S(2)}) async-start(), calls=%async_computation.1 | async-start | bytes 10027008 | tf_op jit(solution)/shard_map/all_gather | solution.py:59
  14.7 95.8 %all-to-all-start = ((bf16[16,9,7168]{2,1,0:T(8,128)(2,1)}), bf16[16,9,7168]{2,1,0:T(8,128)(2,1)}, u32[]{:S(2)}, u32[]{:S(2)}) async-start(bf16[16,9,7168]{2,1,0:T(8,128)(2,1)} %bitcast.45), calls=%async_computation | async-start | bytes 7340032 | tf_op jit(solution)/shard_map/all_to_all | solution.py:39
  23.8 6.7 %copy-start.4 = (s32[128,1]{0,1:T(1,128)S(1)}, s32[128,1]{0,1:T(1,128)}, u32[]{:S(2)}) copy-start(s32[128,1]{0,1:T(1,128)} %param.12) | copy-start | bytes 1540
  23.8 7.0 %copy-start.5 = (u32[256]{0:T(256)S(1)}, u32[256]{0:T(256)}, u32[]{:S(2)}) copy-start(u32[256]{0:T(256)} %constant.43) | copy-start | bytes 3076
  23.8 8.2 %copy-start.3 = (s32[1,2]{1,0:T(1,128)S(1)}, s32[1,2]{1,0:T(1,128)}, u32[]{:S(2)}) copy-start(s32[1,2]{1,0:T(1,128)} %param.15) | copy-start | bytes 28
  30.5 82.8 %copy-start.1 = (f32[128,1]{0,1:T(1,128)S(1)}, f32[128,1]{0,1:T(1,128)}, u32[]{:S(2)}) copy-start(f32[128,1]{0,1:T(1,128)} %param.13) | copy-start | bytes 1540
  115.2 105.9 %copy-start.2 = (s32[1,16]{1,0:T(1,128)S(1)}, s32[1,16]{1,0:T(1,128)}, u32[]{:S(2)}) copy-start(s32[1,16]{1,0:T(1,128)} %param.11) | copy-start | bytes 196
  226.2 2.3 copy-start
Sparse Core Ops, SparseCore 0:
  11.3 76.2 all-gather.6
  90.3 130.7 all-gather.4
where the time goes:
time: 278 us
  waiting for transfers between devices  103 us (37%)
  blocking collectives  77.9 us (28%)
  matrix products  33.4 us (12%)
  local copies, waits for them, and re-layouts  28.4 us (10%)
  between operations  14.8 us (5%)
  other arithmetic  11.3 us (4%)
  starting transfers between devices  9.14 us (3%)
    all_gather x1, waiting for transfers between devices, shards(): portion = lax.all_gather(held_pages, 'dp', axis=1, tiled=True)  102 us
    unnamed x1, blocking collectives  77.9 us
    unnamed x21, local copies, waits for them, and re-layouts  23.3 us
    dot_general x1, matrix products, attend(): jnp.einsum('thc,kc->htk', query_heads, key_rows, preferred_element_type=j...  13 us
    dot_general x1, matrix products, attend(): jnp.einsum('htk,kc->thc', probabilities, key_rows[:, :LAT], preferred_ele...  12.3 us
    sub x1, other arithmetic, attend(): weights = jnp.exp(scores - largest)  10.6 us
    all_to_all x1, starting transfers between devices, combine(): lax.all_to_all(blocks, 'expert', split_axis=0, concat_axis=0, tiled=True)  9.06 us
  transfers between devices with their start and end apart: 3, of which 1 were waited for; matrix products, arithmetic and copies ran while one was open for 8% of the time, Pallas kernels for 0%

commit v1 on v0

v1 whole, which is shorter than its diff:
```python
import functools

import jax
import jax.numpy as jnp
from jax import lax
from jax.experimental import pallas as pl
from jax.experimental.pallas import tpu as pltpu
from jax.sharding import PartitionSpec as P

EXP_GROUP = 24
LAT = 512
PAIR = 2
LANES = 128

exp2_scale = 0.07216878364870322 * 1.4426950408889634


def pick_pages(pages, index):
    count = index.shape[0]

    def kernel(index_ref, pages_ref, out_ref, sems):
        def move(i):
            return pltpu.make_async_copy(pages_ref.at[index_ref[i]], out_ref.at[i], sems.at[i])

        for i in range(count):
            move(i).start()
        for i in range(count):
            move(i).wait()

    return pl.pallas_call(
        kernel,
        out_shape=jax.ShapeDtypeStruct((count,) + pages.shape[1:], pages.dtype),
        in_specs=[pl.BlockSpec(memory_space=pltpu.SMEM), pl.BlockSpec(memory_space=pl.ANY)],
        out_specs=pl.BlockSpec(memory_space=pl.ANY),
        scratch_shapes=[pltpu.SemaphoreType.DMA((count,))],
        name="pick_pages",
    )(index, pages)


def attend_kernel(step_pairs, width, place_ref, q_ref, own_ref, near_ref, far_ref, out_ref, held, low, high, sems):
    count, page_rows, pair_width = held.shape
    span = low.shape[1]
    shift = span - width
    tokens = own_ref.shape[0]
    half = count * page_rows
    prefix = 2 * half

    @pl.when(pl.program_id(0) == 0)
    def _():
        def start(i, source):
            place = place_ref[1, i]
            pltpu.make_async_copy(source.at[place], held.at[i], sems.at[i]).start()

        for i in range(count):

            @pl.when(place_ref[0, i] == 0)
            def _():
                start(i, near_ref)

            @pl.when(place_ref[0, i] != 0)
            def _():
                start(i, far_ref)

        own = own_ref[...]
        empty = jnp.zeros((tokens, shift), own.dtype)
        low[prefix:, :] = jnp.concatenate([own, empty], axis=1)
        high[prefix:, :] = jnp.concatenate([empty, own], axis=1)
        lane = lax.broadcasted_iota(jnp.int32, (page_rows, span), 1)
        for i in range(count):
            pltpu.make_async_copy(near_ref.at[0], held.at[i], sems.at[i]).wait()
            first = jnp.where(lane < width, held[i, :, :span].astype(jnp.float32), 0.0)
            second = jnp.where(lane >= shift, held[i, :, pair_width - span :].astype(jnp.float32), 0.0)
            evens = pl.ds(i * page_rows, page_rows)
            odds = pl.ds(half + i * page_rows, page_rows)
            low[evens, :] = first.astype(low.dtype)
            high[evens, :] = pltpu.roll(first, shift, 1).astype(low.dtype)
            low[odds, :] = pltpu.roll(second, width, 1).astype(low.dtype)
            high[odds, :] = second.astype(low.dtype)

    contract = (((1,), (1,)), ((), ()))
    rows = step_pairs * tokens
    token = lax.broadcasted_iota(jnp.int32, (rows, tokens), 0) % tokens
    visible = lax.broadcasted_iota(jnp.int32, (rows, tokens), 1) <= token
    for parity, keys in ((0, low), (1, high)):
        offset = parity * (pair_width - span)
        q = jnp.concatenate(
            [q_ref[:, p * pair_width + offset : p * pair_width + offset + span] for p in range(step_pairs)], axis=0
        )
        before = lax.dot_general(q, keys[:prefix, :], contract, preferred_element_type=jnp.float32)
        own = lax.dot_general(q, keys[prefix:, :], contract, preferred_element_type=jnp.float32)
        own = jnp.where(visible, own, -jnp.inf)
        largest = jnp.maximum(jnp.max(before, axis=1, keepdims=True), jnp.max(own, axis=1, keepdims=True))
        before = jnp.exp2((before - largest) * exp2_scale)
        own = jnp.exp2((own - largest) * exp2_scale)
        total = jnp.sum(before, axis=1, keepdims=True) + jnp.sum(own, axis=1, keepdims=True)
        mixed = jnp.dot(before.astype(low.dtype), low[:prefix, :LAT], preferred_element_type=jnp.float32)
        mixed += jnp.dot(own.astype(low.dtype), low[prefix:, :LAT], preferred_element_type=jnp.float32)
        mixed = (mixed / total).astype(out_ref.dtype)
        for p in range(step_pairs):
            head = 2 * p + parity
            out_ref[:, head * LAT : (head + 1) * LAT] = mixed[p * tokens : (p + 1) * tokens]


def attend(queries, own, near, far, place):
    tokens, width = own.shape
    _, page_rows, pair_width = near.shape
    count = place.shape[1]
    span = -(-width // LANES) * LANES
    pairs = queries.shape[1] // pair_width
    step_pairs = 2
    keys = count * page_rows * 2 + tokens
    heads = 2 * pairs
    return pl.pallas_call(
        functools.partial(attend_kernel, step_pairs, width),
        out_shape=jax.ShapeDtypeStruct((tokens, heads * LAT), queries.dtype),
        grid=(pairs // step_pairs,),
        in_specs=[
            pl.BlockSpec(memory_space=pltpu.SMEM),
            pl.BlockSpec((tokens, step_pairs * pair_width), lambda i: (0, i)),
            pl.BlockSpec((tokens, width), lambda i: (0, 0)),
            pl.BlockSpec(memory_space=pl.ANY),
            pl.BlockSpec(memory_space=pl.ANY),
        ],
        out_specs=pl.BlockSpec((tokens, 2 * step_pairs * LAT), lambda i: (0, i)),
        scratch_shapes=[
            pltpu.VMEM((count, page_rows, pair_width), queries.dtype),
            pltpu.VMEM((keys, span), queries.dtype),
            pltpu.VMEM((keys, span), queries.dtype),
            pltpu.SemaphoreType.DMA((count,)),
        ],
        compiler_params=pltpu.CompilerParams(vmem_limit_bytes=40 * 2**20),
        cost_estimate=pl.CostEstimate(
            flops=2 * tokens * heads * keys * (width + LAT),
            bytes_accessed=2 * tokens * heads * (width + LAT),
            transcendentals=tokens * heads * keys,
        ),
        name="attend",
    )(place, queries, own, near, far)


def combine_kernel(parts, slot_ref, gate_ref, rows_ref, out_ref):
    tokens = slot_ref.shape[0]
    depth, part_width = rows_ref.shape
    column = lax.broadcasted_iota(jnp.int32, (tokens, depth), 1)
    first = slot_ref[...] * parts
    picker = jnp.concatenate(
        [(column == first + part).astype(rows_ref.dtype) for part in range(parts)], axis=0
    )
    picked = jnp.dot(picker, rows_ref[...], preferred_element_type=jnp.float32)
    gate = gate_ref[...]
    for part in range(parts):
        out_ref[:, part * part_width : (part + 1) * part_width] = (
            picked[part * tokens : (part + 1) * tokens] * gate
        ).astype(out_ref.dtype)


def combine(slot, gate, arrived, parts):
    tokens = slot.shape[0]
    depth, part_width = arrived.shape
    return pl.pallas_call(
        functools.partial(combine_kernel, parts),
        out_shape=jax.ShapeDtypeStruct((tokens, parts * part_width), arrived.dtype),
        in_specs=[pl.BlockSpec(memory_space=pltpu.VMEM)] * 3,
        out_specs=pl.BlockSpec(memory_space=pltpu.VMEM),
        compiler_params=pltpu.CompilerParams(vmem_limit_bytes=40 * 2**20),
        cost_estimate=pl.CostEstimate(
            flops=2 * parts * tokens * depth * part_width,
            bytes_accessed=2 * (depth + tokens * parts) * part_width,
            transcendentals=0,
        ),
        name="combine",
    )(slot, gate, arrived)


def earlier_same(groups):
    count = groups.shape[0]
    order = jnp.arange(count, dtype=jnp.int32)
    same = (groups[None, :] == groups[:, None]) & (order[None, :] < order[:, None])
    return jnp.sum(same.astype(jnp.int32), axis=1)


def shards(queries, new_latent, held_pages, page_list, token_expert, gate, expert_rows, page_table):
    groups_here = lax.axis_size("expert")
    dp_size = lax.axis_size("dp")
    me = lax.axis_index("dp")
    held_count, page_width = held_pages.shape[1:]
    entry_width = new_latent.shape[1]
    pair_width = 2 * entry_width
    page_rows = page_width // pair_width
    half_of = lambda i: (i // 2) % 2
    seat_of = lambda i: (i // 4) * 2 + i % 2
    halves = [[i for i in range(dp_size) if half_of(i) == z] for z in range(2)]
    across = [(i, i ^ 2) for i in range(dp_size)]
    seats = dp_size // 2

    raw = held_pages[0]
    raw_far = lax.ppermute(raw, "dp", across)

    listed = page_list.reshape(-1)
    count = listed.shape[0]
    lists = lax.all_to_all(
        jnp.broadcast_to(listed[None], (seats, count)), "dp", 0, 0, axis_index_groups=halves, tiled=True
    )

    order = jnp.arange(count, dtype=jnp.int32)

    def chosen(holder):
        mine = (lists // held_count) == holder
        rank = jnp.sum((mine[:, None, :] & (order[None, None, :] < order[None, :, None])).astype(jnp.int32), axis=2)
        slots = jnp.arange(PAIR, dtype=jnp.int32)
        hit = mine[:, None, :] & (rank[:, None, :] == slots[None, :, None])
        return jnp.sum(jnp.where(hit, (lists % held_count)[:, None, :], 0), axis=2).reshape(-1)

    def deliver(pages, holder):
        picked = pick_pages(pages.reshape(held_count, page_rows, pair_width), chosen(holder))
        blocks = picked.reshape(seats, PAIR * page_rows, pair_width)
        arrived = lax.all_to_all(blocks, "dp", 0, 0, axis_index_groups=halves, tiled=True)
        return arrived.reshape(seats * PAIR, page_rows, pair_width)

    near = deliver(raw, me)

    capacity, width = expert_rows.shape[3:]
    parts = 8
    blocks = expert_rows.reshape(groups_here, capacity * parts, width // parts)
    blocks, lists = lax.optimization_barrier((blocks, lists))
    arrived = lax.all_to_all(blocks, "expert", 0, 0, tiled=True)

    far = deliver(raw_far, me ^ 2)

    holders = listed // held_count
    rank = jnp.minimum(earlier_same(holders), PAIR - 1)
    place = jnp.stack([(half_of(holders) != half_of(me)).astype(jnp.int32), seat_of(holders) * PAIR + rank])
    context = attend(queries, new_latent, near, far, place)

    groups = (token_expert // EXP_GROUP).reshape(-1)
    slot = groups * capacity + earlier_same(groups)
    moe_out = combine(
        slot[:, None], gate, arrived.reshape(groups_here * capacity * parts, width // parts), parts
    )

    new_count = page_table.shape[1]
    tags = jnp.broadcast_to(page_table.reshape(new_count, 1).astype(new_latent.dtype), (new_count, LANES))
    tagged = jnp.concatenate([new_latent.reshape(new_count, page_width), tags], axis=1)
    pages = lax.all_gather(tagged, "dp", axis=0, tiled=True)
    targets = pages[:, page_width].astype(jnp.int32)
    wanted = me * new_count + jnp.arange(new_count, dtype=jnp.int32)
    picker = (wanted[:, None] == targets[None, :]).astype(pages.dtype)
    slots = jnp.dot(picker, pages[:, :page_width], preferred_element_type=jnp.float32)
    decode_pool = slots.astype(pages.dtype).reshape(1, new_count, page_width)
    return (context, moe_out, decode_pool)


def solution(mesh):
    return jax.shard_map(
        shards,
        mesh=mesh,
        in_specs=(
            P(("expert", "dp"), None),
            P(("expert", "dp"), None),
            P("expert", "dp", None),
            P(("expert", "dp"), None),
            P(("expert", "dp"), None),
            P(("expert", "dp"), None),
            P("expert", "dp", None, None, None),
            P("expert", "dp"),
        ),
        out_specs=(P(("expert", "dp"), None), P(("expert", "dp"), None), P("expert", "dp", None)),
        check_vma=False,
    )
```

time: 278 us -> 249 us (0.90)
  the two profiles are of different devices: /device:TPU:1 before, /device:TPU:64 now
where the time goes in v1:
time: 249 us; the launch traced here: 248 us
  Pallas kernels  104 us (42%)
  waiting for transfers between devices  67 us (27%)
  local copies, waits for them, and re-layouts  28.2 us (11%)
  starting transfers between devices  25.9 us (10%)
  between operations  14.2 us (6%)
  other arithmetic  6.32 us (3%)
  matrix products  2.82 us (1%)
    pallas_call x2, Pallas kernels, pick_pages(): pl.pallas_call(kernel, out_shape=jax.ShapeDtypeStruct((count,) + pages.sh...  75.4 us
    ppermute x1, waiting for transfers between devices, shards(): raw_far = lax.ppermute(raw, 'dp', across)  25.9 us
    all_to_all x1, waiting for transfers between devices, shards(): arrived = lax.all_to_all(blocks, 'expert', 0, 0, tiled=True)  24.6 us
    pallas_call x1, Pallas kernels, attend(): pl.pallas_call(functools.partial(attend_kernel, step_pairs, width), out_s...  24.4 us
    unnamed x21, local copies, waits for them, and re-layouts  17.5 us
    all_to_all x2, waiting for transfers between devices, deliver(): lax.all_to_all(blocks, 'dp', 0, 0, axis_index_groups=halves, tiled=True)  16.4 us
    all_to_all x2, starting transfers between devices, deliver(): lax.all_to_all(blocks, 'dp', 0, 0, axis_index_groups=halves, tiled=True)  9.25 us
    all_to_all x1, starting transfers between devices, shards(): arrived = lax.all_to_all(blocks, 'expert', 0, 0, tiled=True)  6.68 us
  transfers between devices with their start and end apart: 6, of which 3 were waited for; matrix products, arithmetic and copies ran while one was open for 9% of the time, Pallas kernels for 27%

profile of v1, /device:TPU:64, one launch (start us, length us, event | category | flops | bytes accessed | tf_op | source)
XLA Modules:
  0.0 248.3 jit_solution(11970222481739813179)
XLA Ops:
  7.2 1.3 broadcast_in_dim.24
  8.4 4.5 %all-to-all-start = ((s32[8,1,16]{2,1,0:T(1,128)}), s32[8,1,16]{2,1,0:T(1,128)S(1)}, u32[]{:S(2)}, u32[]{:S(2)}) async-start(s32[8,1,16]{2,1,0:T(1,128)} %broadcast_in_dim.24), calls=%async_computation | async-start | bytes 8192 | tf_op jit(solution)/shard_map/all_to_all | solution.py:201
  12.9 1.9 copy.101
  14.8 4.8 %copy.79 = bf16[1,1,16,9,7168]{4,3,2,1,0:T(8,128)(2,1)} copy(bf16[1,1,16,9,7168]{4,2,3,1,0:T(8,128)(2,1)} %param.14) | data formatting | bytes 4128768 | tf_op args[6]
  19.6 5.4 %reshape.131 = bf16[16,72,896]{2,1,0:T(8,128)(2,1)} reshape(bf16[1,1,16,9,7168]{4,3,2,1,0:T(8,128)(2,1)} %copy.79) | data formatting | bytes 4128768 | tf_op jit(solution)/shard_map/reshape | solution.py:224
  26.3 37.8 %pick_pages.2 = bf16[16,32,1152]{2,1,0:T(8,128)(2,1)} custom-call(s32[16]{0:T(128)} %reshape.128.index_ref, bf16[8,32,1152]{2,1,0:T(8,128)(2,1)} %bitcast.41), custom_call_target="tpu_custom_call" | custom-call | tf_op jit(solution)/shard_map/pick_pages/pallas_call | solution.py:30
  64.1 4.8 %all-to-all-start.1 = ((bf16[8,64,1152]{2,1,0:T(8,128)(2,1)}), bf16[8,64,1152]{2,1,0:T(8,128)(2,1)S(1)}, u32[]{:S(2)}, u32[]{:S(2)}) async-start(bf16[8,64,1152]{2,1,0:T(8,128)(2,1)} %bitcast.39), calls=%async_computation.1 | async-start | bytes 2359296 | tf_op jit(solution)/shard_map/all_to_all | solution.py:217
  68.9 5.5 %collective-permute-start = (bf16[8,36864]{1,0:T(8,128)(2,1)S(1)}, bf16[8,36864]{1,0:T(8,128)(2,1)S(1)}, u32[]{:S(2)}, u32[]{:S(2)}) collective-permute-start(bf16[8,36864]{1,0:T(8,128)(2,1)S(1)} %bitcast.44), channel_id=1, source_target_pairs={{0,2},{1,3},{2,0},{3,1},{4,6},{5,7},{6,4},{7,5},{8,10},{9,11},{10,... | collective-permute-start | bytes 1769480 | tf_op jit(solution)/shard_map/ppermute | solution.py:197
  75.4 25.9 %collective-permute-done = bf16[8,36864]{1,0:T(8,128)(2,1)S(1)} collective-permute-done((bf16[8,36864]{1,0:T(8,128)(2,1)S(1)}, bf16[8,36864]{1,0:T(8,128)(2,1)S(1)}, u32[]{:S(2)}, u32[]{:S(2)}) %collective-permute-start) | collective-permute-done | bytes 589856 | tf_op jit(solution)/shard_map/ppermute | solution.py:197
  101.3 0.9 copy.100
  102.2 37.6 %pick_pages.3 = bf16[16,32,1152]{2,1,0:T(8,128)(2,1)} custom-call(s32[16]{0:T(128)} %reshape.132.index_ref, bf16[8,32,1152]{2,1,0:T(8,128)(2,1)} %bitcast.42), custom_call_target="tpu_custom_call" | custom-call | tf_op jit(solution)/shard_map/pick_pages/pallas_call | solution.py:30
  139.9 4.4 %all-to-all-start.2 = ((bf16[8,64,1152]{2,1,0:T(8,128)(2,1)}), bf16[8,64,1152]{2,1,0:T(8,128)(2,1)S(1)}, u32[]{:S(2)}, u32[]{:S(2)}) async-start(bf16[8,64,1152]{2,1,0:T(8,128)(2,1)} %bitcast.40), calls=%async_computation.2 | async-start | bytes 2359296 | tf_op jit(solution)/shard_map/all_to_all | solution.py:217
  144.4 0.8 maximum_bitcast_fusion
  145.2 16.4 %all-to-all-done.2 = bf16[8,64,1152]{2,1,0:T(8,128)(2,1)S(1)} async-done(((bf16[8,64,1152]{2,1,0:T(8,128)(2,1)}), bf16[8,64,1152]{2,1,0:T(8,128)(2,1)S(1)}, u32[]{:S(2)}, u32[]{:S(2)}) %all-to-all-start.2) | async-done | bytes 1179680 | tf_op jit(solution)/shard_map/all_to_all | solution.py:217
  161.7 1.0 copy-done
  162.7 6.7 %all-to-all-start.3 = ((bf16[16,72,896]{2,1,0:T(8,128)(2,1)}), bf16[16,72,896]{2,1,0:T(8,128)(2,1)S(1)}, u32[]{:S(2)}, u32[]{:S(2)}) async-start(bf16[16,72,896]{2,1,0:T(8,128)(2,1)} %reshape.131), calls=%async_computation.3 | async-start | bytes 4128768 | tf_op jit(solution)/shard_map/all_to_all | solution.py:226
  169.6 0.7 copy.86
  170.4 0.7 copy.87
  171.1 0.8 copy.90.gate_ref
  171.9 1.5 fusion.20
  173.6 0.8 copy.89
  174.4 0.7 and_select_fusion
  175.0 0.7 compare_convert_fusion
  175.9 0.9 multiply_add_fusion.slot_ref
  176.8 1.3 copy-done.1
  178.1 2.3 copy-done.2
  180.4 24.4 %attend.1 = bf16[128,16384]{1,0:T(8,128)(2,1)} custom-call(s32[2,16]{1,0:T(2,128)S(1)} %pad_add_fusion.place_ref, bf16[128,18432]{1,0:T(8,128)(2,1)S(1)} %copy-done.2, bf16[128,576]{1,0:T(8,128)(2,1)S(1)} %copy.81.own_ref, bf16[16,32,1152]{2,1,0:T(8,128)(2,1)S(1)} %bitcast.37, bf16[16,32,1152]{2,1,0:T(8,128)(2,1)S(1)} %bitcast.38), custom_call_target="tpu_custom_call" | custom-call | flops 10267656192 | bytes 8912896 | tf_op jit(solution)/shard_map/attend/pallas_call | solution.py:113
  204.8 24.6 %all-to-all-done.3 = bf16[16,72,896]{2,1,0:T(8,128)(2,1)S(1)} async-done(((bf16[16,72,896]{2,1,0:T(8,128)(2,1)}), bf16[16,72,896]{2,1,0:T(8,128)(2,1)S(1)}, u32[]{:S(2)}, u32[]{:S(2)}) %all-to-all-start.3) | async-done | bytes 2064416 | tf_op jit(solution)/shard_map/all_to_all | solution.py:226
  229.5 4.1 %combine.1 = bf16[128,7168]{1,0:T(8,128)(2,1)} custom-call(s32[128,1]{1,0:T(8,128)S(1)} %multiply_add_fusion.slot_ref, f32[128,1]{1,0:T(8,128)S(1)} %copy.90.gate_ref, bf16[1152,896]{1,0:T(8,128)(2,1)S(1)} %bitcast.36), custom_call_target="tpu_custom_call" | custom-call | flops 2113929216 | bytes 3899392 | tf_op jit(solution)/shard_map/combine/pallas_call | solution.py:160
  233.5 4.3 %reshape.141 = bf16[32,36992]{1,0:T(8,128)(2,1)} reshape(bf16[16,2,36992]{2,1,0:T(2,128)(2,1)} %all-gather.3.cloned.1.call-done) | data formatting | bytes 4734976
  237.8 0.8 convert_reduce_fusion.3
  238.6 2.8 %fusion = bf16[1,2,36864]{2,1,0:T(2,128)(2,1)} fusion(bf16[32,36992]{1,0:T(8,128)(2,1)} %reshape.141, s32[32]{0:T(128)S(1)} %convert_reduce_fusion.3, s32[2]{0:T(128)S(1)} %iota_add_fusion), kind=kOutput, calls=%fused_computation.1 | convolution fusion | flops 4792384 | bytes 2506888 | tf_op jit(solution)/shard_map/dot_general | solution.py:248
  (40 shorter events, 3.1 us)
Async XLA Ops:
  8.4 16.6 %all-to-all-start = ((s32[8,1,16]{2,1,0:T(1,128)}), s32[8,1,16]{2,1,0:T(1,128)S(1)}, u32[]{:S(2)}, u32[]{:S(2)}) async-start(s32[8,1,16]{2,1,0:T(1,128)} %broadcast_in_dim.24), calls=%async_computation | async-start | bytes 8192 | tf_op jit(solution)/shard_map/all_to_all | solution.py:201
  25.0 43.9 %copy-start.3 = (bf16[1,8,36864]{2,1,0:T(8,128)(2,1)S(1)}, bf16[1,8,36864]{2,1,0:T(8,128)(2,1)}, u32[]{:S(2)}) copy-start(bf16[1,8,36864]{2,1,0:T(8,128)(2,1)} %param.10) | copy-start | bytes 1769476
  25.0 49.4 %copy-start.4 = (bf16[128,576]{0,1:T(8,128)(2,1)S(1)}, bf16[128,576]{0,1:T(8,128)(2,1)}, u32[]{:S(2)}) copy-start(bf16[128,576]{0,1:T(8,128)(2,1)} %param.9) | copy-start | bytes 442372
  26.3 48.5 %copy-start.6 = (s32[1,2]{1,0:T(1,128)S(1)}, s32[1,2]{1,0:T(1,128)}, u32[]{:S(2)}) copy-start(s32[1,2]{1,0:T(1,128)} %param.15) | copy-start | bytes 28
  64.1 75.8 %all-to-all-start.1 = ((bf16[8,64,1152]{2,1,0:T(8,128)(2,1)}), bf16[8,64,1152]{2,1,0:T(8,128)(2,1)S(1)}, u32[]{:S(2)}, u32[]{:S(2)}) async-start(bf16[8,64,1152]{2,1,0:T(8,128)(2,1)} %bitcast.39), calls=%async_computation.1 | async-start | bytes 2359296 | tf_op jit(solution)/shard_map/all_to_all | solution.py:217
  68.9 32.4 %collective-permute-start = (bf16[8,36864]{1,0:T(8,128)(2,1)S(1)}, bf16[8,36864]{1,0:T(8,128)(2,1)S(1)}, u32[]{:S(2)}, u32[]{:S(2)}) collective-permute-start(bf16[8,36864]{1,0:T(8,128)(2,1)S(1)} %bitcast.44), channel_id=1, source_target_pairs={{0,2},{1,3},{2,0},{3,1},{4,6},{5,7},{6,4},{7,5},{8,10},{9,11},{10,... | collective-permute-start | bytes 1769480 | tf_op jit(solution)/shard_map/ppermute | solution.py:197
  139.9 21.8 %all-to-all-start.2 = ((bf16[8,64,1152]{2,1,0:T(8,128)(2,1)}), bf16[8,64,1152]{2,1,0:T(8,128)(2,1)S(1)}, u32[]{:S(2)}, u32[]{:S(2)}) async-start(bf16[8,64,1152]{2,1,0:T(8,128)(2,1)} %bitcast.40), calls=%async_computation.2 | async-start | bytes 2359296 | tf_op jit(solution)/shard_map/all_to_all | solution.py:217
  144.3 25.1 %copy-start.5 = (s32[128,1]{0,1:T(1,128)S(1)}, s32[128,1]{0,1:T(1,128)}, u32[]{:S(2)}) copy-start(s32[128,1]{0,1:T(1,128)} %param.12) | copy-start | bytes 1540
  144.3 89.2 %all-gather.3.cloned.1.call-start = ((), (), s32[]{:S(2)}) async-start(), calls=%async_computation.4 | async-start | bytes 2515456 | tf_op jit(solution)/shard_map/all_gather | solution.py:244
  161.7 1.0 copy-start
  162.7 66.8 %all-to-all-start.3 = ((bf16[16,72,896]{2,1,0:T(8,128)(2,1)}), bf16[16,72,896]{2,1,0:T(8,128)(2,1)S(1)}, u32[]{:S(2)}, u32[]{:S(2)}) async-start(bf16[16,72,896]{2,1,0:T(8,128)(2,1)} %reshape.131), calls=%async_computation.3 | async-start | bytes 4128768 | tf_op jit(solution)/shard_map/all_to_all | solution.py:226
  176.8 1.3 copy-start.1
  178.1 2.3 copy-start.2
Sparse Core Ops, SparseCore 0:
  147.9 66.3 all-gather.2

commit v2 on v1

v2 whole, which is shorter than its diff:
```python
import functools

import jax
import jax.numpy as jnp
from jax import lax
from jax.experimental import pallas as pl
from jax.experimental.pallas import tpu as pltpu
from jax.sharding import PartitionSpec as P

EXP_GROUP = 24
LAT = 512
PAIR = 2
LANES = 128

exp2_scale = 0.07216878364870322 * 1.4426950408889634


def pick_kernel(index_ref, *refs):
    page_refs, out_ref = refs[:-1], refs[-1]
    each, count = len(page_refs), index_ref.shape[0]
    for i in range(count):
        out_ref[i] = page_refs[i // PAIR % each][index_ref[i], : out_ref.shape[1]]


def pick_pages(sources, index, rows=None):
    width = sources[0].shape[2]
    rows = rows or sources[0].shape[1]
    return pl.pallas_call(
        pick_kernel,
        out_shape=jax.ShapeDtypeStruct((index.shape[0], rows, width), sources[0].dtype),
        in_specs=[pl.BlockSpec(memory_space=pltpu.SMEM)] + [pl.BlockSpec(memory_space=pltpu.VMEM)] * len(sources),
        out_specs=pl.BlockSpec(memory_space=pltpu.VMEM),
        compiler_params=pltpu.CompilerParams(vmem_limit_bytes=16 * 2**20),
        name="pick_pages",
    )(index, *sources)


def attend_kernel(step_pairs, width, blocks, place_ref, q_ref, own_ref, *refs):
    block_refs, (out_ref, held, low, high, sems) = refs[:blocks], refs[blocks:]
    count = place_ref.shape[0]
    each, page_rows, pair_width = block_refs[0].shape
    span = low.shape[1]
    shift = span - width
    tokens = own_ref.shape[0]
    half = count * page_rows
    prefix = 2 * half

    @pl.when(pl.program_id(0) == 0)
    def _():
        def move(i):
            return pltpu.make_async_copy(block_refs[i], held.at[pl.ds(each * i, each)], sems.at[i])

        for i in range(blocks):
            move(i).start()

        own = own_ref[...]
        empty = jnp.zeros((tokens, shift), own.dtype)
        low[prefix:, :] = jnp.concatenate([own, empty], axis=1)
        high[prefix:, :] = jnp.concatenate([empty, own], axis=1)
        lane = lax.broadcasted_iota(jnp.int32, (page_rows, span), 1)
        for i in range(blocks):
            move(i).wait()
        for i in range(count):
            place = place_ref[i]
            first = jnp.where(lane < width, held[place, :, :span].astype(jnp.float32), 0.0)
            second = jnp.where(lane >= shift, held[place, :, pair_width - span :].astype(jnp.float32), 0.0)
            evens = pl.ds(i * page_rows, page_rows)
            odds = pl.ds(half + i * page_rows, page_rows)
            low[evens, :] = first.astype(low.dtype)
            high[evens, :] = pltpu.roll(first, shift, 1).astype(low.dtype)
            low[odds, :] = pltpu.roll(second, width, 1).astype(low.dtype)
            high[odds, :] = second.astype(low.dtype)

    contract = (((1,), (1,)), ((), ()))
    rows = step_pairs * tokens
    token = lax.broadcasted_iota(jnp.int32, (rows, tokens), 0) % tokens
    visible = lax.broadcasted_iota(jnp.int32, (rows, tokens), 1) <= token
    for parity, keys in ((0, low), (1, high)):
        offset = parity * (pair_width - span)
        q = jnp.concatenate(
            [q_ref[:, p * pair_width + offset : p * pair_width + offset + span] for p in range(step_pairs)], axis=0
        )
        before = lax.dot_general(q, keys[:prefix, :], contract, preferred_element_type=jnp.float32)
        own = lax.dot_general(q, keys[prefix:, :], contract, preferred_element_type=jnp.float32)
        own = jnp.where(visible, own, -jnp.inf)
        largest = jnp.maximum(jnp.max(before, axis=1, keepdims=True), jnp.max(own, axis=1, keepdims=True))
        before = jnp.exp2((before - largest) * exp2_scale)
        own = jnp.exp2((own - largest) * exp2_scale)
        total = jnp.sum(before, axis=1, keepdims=True) + jnp.sum(own, axis=1, keepdims=True)
        mixed = jnp.dot(before.astype(low.dtype), low[:prefix, :LAT], preferred_element_type=jnp.float32)
        mixed += jnp.dot(own.astype(low.dtype), low[prefix:, :LAT], preferred_element_type=jnp.float32)
        mixed = (mixed / total).astype(out_ref.dtype)
        for p in range(step_pairs):
            head = 2 * p + parity
            out_ref[:, head * LAT : (head + 1) * LAT] = mixed[p * tokens : (p + 1) * tokens]


def attend(queries, own, blocks, place):
    tokens, width = own.shape
    _, page_rows, pair_width = blocks[0].shape
    count = place.shape[0]
    span = -(-width // LANES) * LANES
    pairs = queries.shape[1] // pair_width
    step_pairs = 4
    keys = count * page_rows * 2 + tokens
    heads = 2 * pairs
    return pl.pallas_call(
        functools.partial(attend_kernel, step_pairs, width, len(blocks)),
        out_shape=jax.ShapeDtypeStruct((tokens, heads * LAT), queries.dtype),
        grid=(pairs // step_pairs,),
        in_specs=[
            pl.BlockSpec(memory_space=pltpu.SMEM),
            pl.BlockSpec((tokens, step_pairs * pair_width), lambda i: (0, i)),
            pl.BlockSpec((tokens, width), lambda i: (0, 0)),
        ]
        + [pl.BlockSpec(memory_space=pl.ANY)] * len(blocks),
        out_specs=pl.BlockSpec((tokens, 2 * step_pairs * LAT), lambda i: (0, i)),
        scratch_shapes=[
            pltpu.VMEM((len(blocks) * blocks[0].shape[0], page_rows, pair_width), queries.dtype),
            pltpu.VMEM((keys, span), queries.dtype),
            pltpu.VMEM((keys, span), queries.dtype),
            pltpu.SemaphoreType.DMA((len(blocks),)),
        ],
        compiler_params=pltpu.CompilerParams(vmem_limit_bytes=56 * 2**20),
        cost_estimate=pl.CostEstimate(
            flops=2 * tokens * heads * keys * (width + LAT),
            bytes_accessed=2 * tokens * heads * (width + LAT),
            transcendentals=tokens * heads * keys,
        ),
        name="attend",
    )(place, queries, own, *blocks)


def pack_kernel(groups, parts, here_ref, rows_ref, *refs):
    out_refs, stack = refs[:-1], refs[-1]
    count, width = rows_ref.shape
    part_width = width // parts
    for part in range(parts):
        stack[pl.ds(part * count, count), :] = rows_ref[:, part * part_width : (part + 1) * part_width]
    side = len(out_refs)
    block = count // groups * parts
    depth = parts * count
    row = lax.broadcasted_iota(jnp.int32, (side * block, 1), 0)
    k = row // block
    slot = (row - k * block) // parts
    part = row % parts
    column = lax.broadcasted_iota(jnp.int32, (side * block, depth), 1)
    for far in range(side):
        group = (k * side + far) ^ here_ref[0]
        picker = (column == part * count + slot * groups + group).astype(stack.dtype)
        out_refs[far][...] = jnp.dot(picker, stack[...], preferred_element_type=jnp.float32).astype(stack.dtype)


def pack_rows(rows, here, groups, side, parts):
    count, width = rows.shape
    out = jax.ShapeDtypeStruct((count * parts // side, width // parts), rows.dtype)
    return pl.pallas_call(
        functools.partial(pack_kernel, groups, parts),
        out_shape=(out,) * side,
        in_specs=[pl.BlockSpec(memory_space=pltpu.SMEM), pl.BlockSpec(memory_space=pltpu.VMEM)],
        out_specs=(pl.BlockSpec(memory_space=pltpu.VMEM),) * side,
        scratch_shapes=[pltpu.VMEM((count * parts, width // parts), rows.dtype)],
        compiler_params=pltpu.CompilerParams(vmem_limit_bytes=32 * 2**20),
        cost_estimate=pl.CostEstimate(
            flops=2 * count * parts * count * width, bytes_accessed=4 * count * width, transcendentals=0
        ),
        name="pack_rows",
    )(here, rows)


def turn_kernel(*refs):
    side = len(refs) // 2
    share = refs[0].shape[0] // side
    for k in range(side):
        for far in range(side):
            refs[side + k][pl.ds(far * share, share), :] = refs[far][pl.ds(k * share, share), :]


def turn(blocks):
    side = len(blocks)
    return pl.pallas_call(
        turn_kernel,
        out_shape=(jax.ShapeDtypeStruct(blocks[0].shape, blocks[0].dtype),) * side,
        in_specs=[pl.BlockSpec(memory_space=pltpu.VMEM)] * side,
        out_specs=(pl.BlockSpec(memory_space=pltpu.VMEM),) * side,
        compiler_params=pltpu.CompilerParams(vmem_limit_bytes=16 * 2**20),
        name="turn",
    )(*blocks)


def combine_kernel(parts, slot_ref, gate_ref, *refs):
    row_refs, (out_ref, rows, sems) = refs[:-3], refs[-3:]
    tokens = slot_ref.shape[0]
    depth, part_width = rows.shape
    share = row_refs[0].shape[0]

    def move(i):
        return pltpu.make_async_copy(row_refs[i], rows.at[pl.ds(i * share, share)], sems.at[i])

    for i in range(len(row_refs)):
        move(i).start()
    column = lax.broadcasted_iota(jnp.int32, (tokens, depth), 1)
    first = slot_ref[...] * parts
    picker = jnp.concatenate([(column == first + part).astype(rows.dtype) for part in range(parts)], axis=0)
    gate = gate_ref[...]
    for i in range(len(row_refs)):
        move(i).wait()
    picked = jnp.dot(picker, rows[...], preferred_element_type=jnp.float32)
    for part in range(parts):
        out_ref[:, part * part_width : (part + 1) * part_width] = (
            picked[part * tokens : (part + 1) * tokens] * gate
        ).astype(out_ref.dtype)


def combine(slot, gate, arrived, parts):
    tokens = slot.shape[0]
    depth = sum(block.shape[0] for block in arrived)
    part_width = arrived[0].shape[1]
    return pl.pallas_call(
        functools.partial(combine_kernel, parts),
        out_shape=jax.ShapeDtypeStruct((tokens, parts * part_width), arrived[0].dtype),
        in_specs=[pl.BlockSpec(memory_space=pltpu.VMEM)] * 2 + [pl.BlockSpec(memory_space=pl.ANY)] * len(arrived),
        out_specs=pl.BlockSpec(memory_space=pltpu.VMEM),
        scratch_shapes=[
            pltpu.VMEM((depth, part_width), arrived[0].dtype),
            pltpu.SemaphoreType.DMA((len(arrived),)),
        ],
        compiler_params=pltpu.CompilerParams(vmem_limit_bytes=40 * 2**20),
        cost_estimate=pl.CostEstimate(
            flops=2 * parts * tokens * depth * part_width,
            bytes_accessed=2 * (depth + tokens * parts) * part_width,
            transcendentals=0,
        ),
        name="combine",
    )(slot, gate, *arrived)


def earlier_same(groups):
    count = groups.shape[0]
    order = jnp.arange(count, dtype=jnp.int32)
    same = (groups[None, :] == groups[:, None]) & (order[None, :] < order[:, None])
    return jnp.sum(same.astype(jnp.int32), axis=1)


def first_match(wanted, values):
    hit = wanted[:, None] == values[None, :]
    order = jnp.arange(values.shape[0], dtype=jnp.int32)
    first = jnp.min(jnp.where(hit, order[None, :], values.shape[0]), axis=1)
    return jnp.where(first < values.shape[0], first, 0)


def shards(queries, new_latent, held_pages, page_list, token_expert, gate, expert_rows, page_table):
    groups_here = lax.axis_size("expert")
    dp_size = lax.axis_size("dp")
    me = lax.axis_index("dp")
    held_count, page_width = held_pages.shape[1:]
    entry_width = new_latent.shape[1]
    pair_width = 2 * entry_width
    page_rows = page_width // pair_width
    half_of = lambda i: (i // 2) % 2
    seat_of = lambda i: (i // 4) * 2 + i % 2
    halves = [[i for i in range(dp_size) if half_of(i) == z] for z in range(2)]
    across = [(i, i ^ 2) for i in range(dp_size)]
    seats = dp_size // 2

    raw = held_pages[0]
    raw_far = lax.ppermute(raw, "dp", across)

    listed = page_list.reshape(-1)
    count = listed.shape[0]
    here = lax.axis_index("expert")
    capacity, width = expert_rows.shape[3:]
    parts = 8
    side = 4
    along = lambda k: [(i, i ^ k) for i in range(groups_here)]
    rows = jnp.transpose(expert_rows[0, 0], (1, 0, 2)).reshape(capacity * groups_here, width)
    packed = pack_rows(rows, here.reshape(1).astype(jnp.int32), groups_here, side, parts)
    packed, listed = lax.optimization_barrier((packed, listed))
    lists = lax.all_to_all(
        jnp.broadcast_to(listed[None], (seats, count)), "dp", 0, 0, axis_index_groups=halves, tiled=True
    )

    order = jnp.arange(count, dtype=jnp.int32)
    mine = (lists // held_count)[:, None, :] == jnp.stack([me, me ^ 2])[None, :, None]
    rank = jnp.sum((mine[:, :, None, :] & (order[None, :] < order[:, None])).astype(jnp.int32), axis=3)
    slots = jnp.arange(PAIR, dtype=jnp.int32)
    hit = mine[:, :, None, :] & (rank[:, :, None, :] == slots[:, None])
    chosen = jnp.sum(jnp.where(hit, (lists % held_count)[:, None, None, :], 0), axis=3).reshape(-1)

    def deliver(picked):
        blocks = picked.reshape(seats, -1, picked.shape[2])
        arrived = lax.all_to_all(blocks, "dp", 0, 0, axis_index_groups=halves, tiled=True)
        return arrived.reshape(picked.shape)

    met = [packed[0]] + [lax.ppermute(packed[far], "expert", along(far)) for far in range(1, side)]
    page_shape = (held_count, page_rows, pair_width)
    raw_far, met[1] = lax.optimization_barrier((raw_far, met[1]))
    listed_pages = deliver(pick_pages((raw.reshape(page_shape), raw_far.reshape(page_shape)), chosen))

    new_count = page_table.shape[1]
    page_tiles = page_width // LANES
    tags = jnp.broadcast_to(page_table.reshape(new_count, 1, 1).astype(new_latent.dtype), (new_count, 16, LANES))
    tagged = jnp.concatenate([new_latent.reshape(new_count, page_tiles, LANES), tags], axis=1)
    tagged, raw_far = lax.optimization_barrier((tagged, raw_far))
    tagged_far = lax.ppermute(tagged, "dp", across)

    met, tagged_far = lax.optimization_barrier((met, tagged_far))
    turned = turn(met)
    arrived = [turned[0]] + [lax.ppermute(turned[k], "expert", along(k * side)) for k in range(1, side)]

    holders = listed // held_count
    rank = jnp.minimum(earlier_same(holders), PAIR - 1)
    across_half = (half_of(holders) != half_of(me)).astype(jnp.int32)
    place = (seat_of(holders) * 2 + across_half) * PAIR + rank
    context = attend(queries, new_latent, (listed_pages,), place)

    groups = (token_expert // EXP_GROUP).reshape(-1)
    slot = (groups ^ here) * capacity + earlier_same(groups)

    both = jnp.concatenate([tagged, tagged_far], axis=0)
    seat = jnp.arange(seats, dtype=jnp.int32)
    owner = (seat // 2) * 4 + half_of(me) * 2 + seat % 2
    wanted = (owner[:, None] * new_count + jnp.arange(new_count, dtype=jnp.int32)).reshape(-1)
    source = first_match(wanted, both[:, page_tiles, 0].astype(jnp.int32))
    picked = pick_pages((both,), source)
    picked, listed_pages, arrived[3] = lax.optimization_barrier((picked, listed_pages, arrived[3]))
    pages = deliver(picked)
    tagged_as = pages[:, page_tiles, 0].astype(jnp.int32)
    source = first_match(me * new_count + jnp.arange(new_count, dtype=jnp.int32), tagged_as)
    decode_pool = pick_pages((pages,), source, page_tiles).reshape(1, new_count, page_width)
    slot, context, decode_pool = lax.optimization_barrier((slot, context, decode_pool))
    moe_out = combine(slot[:, None], gate, arrived, parts)
    return (context, moe_out, decode_pool)


def solution(mesh):
    return jax.shard_map(
        shards,
        mesh=mesh,
        in_specs=(
            P(("expert", "dp"), None),
            P(("expert", "dp"), None),
            P("expert", "dp", None),
            P(("expert", "dp"), None),
            P(("expert", "dp"), None),
            P(("expert", "dp"), None),
            P("expert", "dp", None, None, None),
            P("expert", "dp"),
        ),
        out_specs=(P(("expert", "dp"), None), P(("expert", "dp"), None), P("expert", "dp", None)),
        check_vma=False,
    )
```

time: 249 us -> 126 us (0.51)
  the two profiles are of different devices: /device:TPU:64 before, /device:TPU:1 now
where the time goes in v2:
time: 126 us; the launch traced here: 124 us
  starting transfers between devices  57.5 us (46%)
  Pallas kernels  34.5 us (27%)
  waiting for transfers between devices  19.9 us (16%)
  local copies, waits for them, and re-layouts  8.74 us (7%)
  other arithmetic  2.54 us (2%)
    pallas_call x1, Pallas kernels, attend(): pl.pallas_call(functools.partial(attend_kernel, step_pairs, width, len(bl...  21.1 us
    all_to_all x2, starting transfers between devices, deliver(): lax.all_to_all(blocks, 'dp', 0, 0, axis_index_groups=halves, tiled=True)  20 us
    ppermute x3, starting transfers between devices, shards(): lax.ppermute(turned[k], 'expert', along(k * side))  13.3 us
    ppermute x3, waiting for transfers between devices, shards(): lax.ppermute(turned[k], 'expert', along(k * side))  11.3 us
    ppermute x1, starting transfers between devices, shards(): raw_far = lax.ppermute(raw, 'dp', across)  6.92 us
    unnamed x31, local copies, waits for them, and re-layouts  6.75 us
    ppermute x1, starting transfers between devices, shards(): tagged_far = lax.ppermute(tagged, 'dp', across)  6.37 us
    all_to_all x1, starting transfers between devices, shards(): lax.all_to_all(jnp.broadcast_to(listed[None], (seats, count)), 'dp', 0, 0...  6.26 us
  transfers between devices with their start and end apart: 11, of which 4 were waited for; matrix products, arithmetic and copies ran while one was open for 6% of the time, Pallas kernels for 21%

profile of v2, /device:TPU:1, one launch (start us, length us, event | category | flops | bytes accessed | tf_op | source)
XLA Modules:
  0.0 124.4 jit_solution(9577202634359340526)
XLA Ops:
  0.6 1.6 %copy-done = bf16[1,1,16,9,7168]{4,2,3,1,0:T(8,128)(2,1)S(1)} copy-done((bf16[1,1,16,9,7168]{4,2,3,1,0:T(8,128)(2,1)S(1)}, bf16[1,1,16,9,7168]{4,2,3,1,0:T(8,128)(2,1)}, u32[]{:S(2)}) %copy-start) | copy-done | bytes 2064408
  2.2 3.4 %pack_rows.1 = (bf16[288,896]{1,0:T(8,128)(2,1)S(1)}, bf16[288,896]{1,0:T(8,128)(2,1)}, bf16[288,896]{1,0:T(8,128)(2,1)}, bf16[288,896]{1,0:T(8,128)(2,1)S(1)}) custom-call(s32[1]{0:T(128)} %bitcast.1.here_ref, bf16[144,7168]{1,0:T(8,128)(2,1)S(1)} %bitcast.38), custom_call_target="tpu_custom_call" | custom-call | flops 2378170368 | bytes 4128768 | tf_op jit(solution)/shard_map/pack_rows/pallas_call | solution.py:157
  5.6 2.1 %collective-permute-start.1 = (bf16[288,896]{1,0:T(8,128)(2,1)}, bf16[288,896]{1,0:T(8,128)(2,1)S(1)}, u32[]{:S(2)}, u32[]{:S(2)}) collective-permute-start(bf16[288,896]{1,0:T(8,128)(2,1)} %get-tuple-element.34), channel_id=1, source_target_pairs={{0,16},{16,0},{32,48},{48,32},{64,80},{80,64},{96,112},{112,96},{1... | collective-permute-start | bytes 1548296 | tf_op jit(solution)/shard_map/ppermute | solution.py:295
  7.7 6.9 %collective-permute-start = (bf16[8,36864]{1,0:T(8,128)(2,1)}, bf16[8,36864]{1,0:T(8,128)(2,1)}, u32[]{:S(2)}, u32[]{:S(2)}) collective-permute-start(bf16[8,36864]{1,0:T(8,128)(2,1)} %bitcast.11), channel_id=1, source_target_pairs={{0,2},{1,3},{2,0},{3,1},{4,6},{5,7},{6,4},{7,5},{8,10},{9,11},{10,... | collective-permute-start | bytes 1769480 | tf_op jit(solution)/shard_map/ppermute | solution.py:267
  14.6 2.4 %collective-permute-start.2 = (bf16[288,896]{1,0:T(8,128)(2,1)}, bf16[288,896]{1,0:T(8,128)(2,1)S(1)}, u32[]{:S(2)}, u32[]{:S(2)}) collective-permute-start(bf16[288,896]{1,0:T(8,128)(2,1)} %get-tuple-element.39), channel_id=1, source_target_pairs={{0,32},{16,48},{32,0},{48,16},{64,96},{80,112},{96,64},{112,80},{1... | collective-permute-start | bytes 1548296 | tf_op jit(solution)/shard_map/ppermute | solution.py:295
  17.2 0.6 broadcast_in_dim.42
  17.8 6.3 %all-to-all-start = ((s32[8,1,16]{2,1,0:T(1,128)}), s32[8,1,16]{2,1,0:T(1,128)S(1)}, u32[]{:S(2)}, u32[]{:S(2)}) async-start(s32[8,1,16]{2,1,0:T(1,128)} %broadcast_in_dim.42), calls=%async_computation | async-start | bytes 8192 | tf_op jit(solution)/shard_map/all_to_all | solution.py:279
  24.2 1.1 copy.43
  25.3 3.7 %all-to-all-done = s32[8,1,16]{2,1,0:T(1,128)S(1)} async-done(((s32[8,1,16]{2,1,0:T(1,128)}), s32[8,1,16]{2,1,0:T(1,128)S(1)}, u32[]{:S(2)}, u32[]{:S(2)}) %all-to-all-start) | async-done | bytes 544 | tf_op jit(solution)/shard_map/all_to_all | solution.py:279
  29.1 0.4 convert_reduce_fusion
  29.8 1.1 copy.42
  31.0 2.1 %pick_pages.3 = bf16[32,32,1152]{2,1,0:T(8,128)(2,1)} custom-call(s32[32]{0:T(128)S(1)} %reshape.157.index_ref, bf16[8,32,1152]{2,1,0:T(8,128)(2,1)S(1)} %bitcast.36, bf16[8,32,1152]{2,1,0:T(8,128)(2,1)S(1)} %bitcast.37), custom_call_target="tpu_custom_call" | custom-call | tf_op jit(solution)/shard_map/pick_pages/pallas_call | solution.py:28
  33.1 15.0 %all-to-all-start.1 = ((bf16[8,128,1152]{2,1,0:T(8,128)(2,1)}), bf16[8,128,1152]{2,1,0:T(8,128)(2,1)}, u32[]{:S(2)}, u32[]{:S(2)}) async-start(bf16[8,128,1152]{2,1,0:T(8,128)(2,1)} %bitcast.12), calls=%async_computation.1 | async-start | bytes 4718592 | tf_op jit(solution)/shard_map/all_to_all | solution.py:292
  48.3 0.2 reshape.161
  48.8 0.5 minimum_add_fusion.place_ref
  49.5 6.4 %collective-permute-start.4 = (bf16[2,304,128]{2,1,0:T(8,128)(2,1)S(1)}, bf16[2,304,128]{2,1,0:T(8,128)(2,1)S(1)}, u32[]{:S(2)}, u32[]{:S(2)}) collective-permute-start(bf16[2,304,128]{2,1,0:T(8,128)(2,1)S(1)} %pad_maximum_fusion), channel_id=1, source_target_pairs={{0,2},{1,3},{2,0},{3,1},{4,6},{5,7},{6,4},{7,5},{8,10},{9,11},{10,... | collective-permute-start | bytes 466952 | tf_op jit(solution)/shard_map/ppermute | solution.py:305
  56.1 4.1 %collective-permute-done.4 = bf16[2,304,128]{2,1,0:T(8,128)(2,1)S(1)} collective-permute-done((bf16[2,304,128]{2,1,0:T(8,128)(2,1)S(1)}, bf16[2,304,128]{2,1,0:T(8,128)(2,1)S(1)}, u32[]{:S(2)}, u32[]{:S(2)}) %collective-permute-start.4) | collective-permute-done | bytes 155680 | tf_op jit(solution)/shard_map/ppermute | solution.py:305
  60.4 0.8 copy-done.3
  61.2 1.3 %collective-permute-start.5 = (bf16[288,896]{1,0:T(8,128)(2,1)S(1)}, bf16[288,896]{1,0:T(8,128)(2,1)S(1)}, u32[]{:S(2)}, u32[]{:S(2)}) collective-permute-start(bf16[288,896]{1,0:T(8,128)(2,1)S(1)} %get-tuple-element.46), channel_id=1, source_target_pairs={{0,192},{16,208},{32,224},{48,240},{64,128},{80,144},{96,160},{112... | collective-permute-start | bytes 1548296 | tf_op jit(solution)/shard_map/ppermute | solution.py:309
  62.8 1.7 %pick_pages.4 = bf16[16,304,128]{2,1,0:T(8,128)(2,1)} custom-call(s32[16]{0:T(128)S(1)} %compare_select_fusion.1.index_ref, bf16[4,304,128]{2,1,0:T(8,128)(2,1)S(1)} %constant_dynamic-update-slice_fusion.refs_0_), custom_call_target="tpu_custom_call" | custom-call | tf_op jit(solution)/shard_map/pick_pages/pallas_call | solution.py:28
  64.4 11.3 %collective-permute-done.5.refs_3_ = bf16[288,896]{1,0:T(8,128)(2,1)S(1)} collective-permute-done((bf16[288,896]{1,0:T(8,128)(2,1)S(1)}, bf16[288,896]{1,0:T(8,128)(2,1)S(1)}, u32[]{:S(2)}, u32[]{:S(2)}) %collective-permute-start.5) | collective-permute-done | bytes 516128 | tf_op jit(solution)/shard_map/ppermute | solution.py:309
  75.7 0.8 copy-done.5
  76.5 0.8 all-to-all-done.1
  77.4 5.0 %all-to-all-start.2 = ((bf16[8,608,128]{2,1,0:T(8,128)(2,1)}), bf16[8,608,128]{2,1,0:T(8,128)(2,1)S(1)}, u32[]{:S(2)}, u32[]{:S(2)}) async-start(bf16[8,608,128]{2,1,0:T(8,128)(2,1)} %bitcast.15), calls=%async_computation.2 | async-start | bytes 2490368 | tf_op jit(solution)/shard_map/all_to_all | solution.py:292
  82.5 11.3 %collective-permute-start.6 = (bf16[288,896]{1,0:T(8,128)(2,1)S(1)}, bf16[288,896]{1,0:T(8,128)(2,1)}, u32[]{:S(2)}, u32[]{:S(2)}) collective-permute-start(bf16[288,896]{1,0:T(8,128)(2,1)S(1)} %copy-done.4), channel_id=1, source_target_pairs={{0,64},{16,80},{32,96},{48,112},{64,0},{80,16},{96,32},{112,48},{1... | collective-permute-start | bytes 1548296 | tf_op jit(solution)/shard_map/ppermute | solution.py:309
  93.8 0.7 collective-permute-start.7
  94.5 21.1 %attend.1 = bf16[128,16384]{1,0:T(8,128)(2,1)} custom-call(s32[16]{0:T(128)} %minimum_add_fusion.place_ref, bf16[128,18432]{1,0:T(8,128)(2,1)} %q_ref.1, bf16[128,576]{1,0:T(8,128)(2,1)} %copy-done.7, bf16[32,32,1152]{2,1,0:T(8,128)(2,1)} %bitcast.13.refs_0_), custom_call_target="tpu_custom_call" | custom-call | flops 10267656192 | bytes 8912896 | tf_op jit(solution)/shard_map/attend/pallas_call | solution.py:107
  115.6 0.4 fusion.2
  116.2 0.6 pick_pages.5
  116.7 0.7 reshape.164
  117.6 1.0 copy-done.6
  118.6 5.6 %combine.1 = bf16[128,7168]{1,0:T(8,128)(2,1)} custom-call(s32[128,1]{1,0:T(8,128)S(1)} %copy.36.slot_ref, f32[128,1]{1,0:T(8,128)S(1)} %copy.37.gate_ref, bf16[288,896]{1,0:T(8,128)(2,1)S(1)} %get-tuple-element.50.refs_0_, bf16[288,896]{1,0:T(8,128)(2,1)} %collective-permute-done.6.refs_1_, bf16[288,896]{1,0:T(8,128)(2,1)} %collective-permute-done.7.refs_2_, ...), custom_call_target="tpu_custom_call" | custom-call | flops 2113929216 | bytes 3899392 | tf_op jit(solution)/shard_map/combine/pallas_call | solution.py:219
  (63 shorter events, 2.5 us)
Async XLA Ops:
  0.6 1.6 %copy-start = (bf16[1,1,16,9,7168]{4,2,3,1,0:T(8,128)(2,1)S(1)}, bf16[1,1,16,9,7168]{4,2,3,1,0:T(8,128)(2,1)}, u32[]{:S(2)}) copy-start(bf16[1,1,16,9,7168]{4,2,3,1,0:T(8,128)(2,1)} %param.14) | copy-start | bytes 6193156
  2.2 15.0 %copy-start.9 = (s32[1,16]{1,0:T(1,128)S(1)}, s32[1,16]{1,0:T(1,128)}, u32[]{:S(2)}) copy-start(s32[1,16]{1,0:T(1,128)} %param.11) | copy-start | bytes 196
  5.6 24.2 %collective-permute-start.1 = (bf16[288,896]{1,0:T(8,128)(2,1)}, bf16[288,896]{1,0:T(8,128)(2,1)S(1)}, u32[]{:S(2)}, u32[]{:S(2)}) collective-permute-start(bf16[288,896]{1,0:T(8,128)(2,1)} %get-tuple-element.34), channel_id=1, source_target_pairs={{0,16},{16,0},{32,48},{48,32},{64,80},{80,64},{96,112},{112,96},{1... | collective-permute-start | bytes 1548296 | tf_op jit(solution)/shard_map/ppermute | solution.py:295
  7.7 22.2 %collective-permute-start = (bf16[8,36864]{1,0:T(8,128)(2,1)}, bf16[8,36864]{1,0:T(8,128)(2,1)}, u32[]{:S(2)}, u32[]{:S(2)}) collective-permute-start(bf16[8,36864]{1,0:T(8,128)(2,1)} %bitcast.11), channel_id=1, source_target_pairs={{0,2},{1,3},{2,0},{3,1},{4,6},{5,7},{6,4},{7,5},{8,10},{9,11},{10,... | collective-permute-start | bytes 1769480 | tf_op jit(solution)/shard_map/ppermute | solution.py:267
  14.6 41.5 %collective-permute-start.2 = (bf16[288,896]{1,0:T(8,128)(2,1)}, bf16[288,896]{1,0:T(8,128)(2,1)S(1)}, u32[]{:S(2)}, u32[]{:S(2)}) collective-permute-start(bf16[288,896]{1,0:T(8,128)(2,1)} %get-tuple-element.39), channel_id=1, source_target_pairs={{0,32},{16,48},{32,0},{48,16},{64,96},{80,112},{96,64},{112,80},{1... | collective-permute-start | bytes 1548296 | tf_op jit(solution)/shard_map/ppermute | solution.py:295
  17.0 39.1 %collective-permute-start.3 = (bf16[288,896]{1,0:T(8,128)(2,1)S(1)}, bf16[288,896]{1,0:T(8,128)(2,1)S(1)}, u32[]{:S(2)}, u32[]{:S(2)}) collective-permute-start(bf16[288,896]{1,0:T(8,128)(2,1)S(1)} %get-tuple-element.40), channel_id=1, source_target_pairs={{0,48},{16,32},{32,16},{48,0},{64,112},{80,96},{96,80},{112,64},{1... | collective-permute-start | bytes 1548296 | tf_op jit(solution)/shard_map/ppermute | solution.py:295
  17.8 11.2 %all-to-all-start = ((s32[8,1,16]{2,1,0:T(1,128)}), s32[8,1,16]{2,1,0:T(1,128)S(1)}, u32[]{:S(2)}, u32[]{:S(2)}) async-start(s32[8,1,16]{2,1,0:T(1,128)} %broadcast_in_dim.42), calls=%async_computation | async-start | bytes 8192 | tf_op jit(solution)/shard_map/all_to_all | solution.py:279
  33.1 15.0 %copy-start.8 = (bf16[128,576]{0,1:T(8,128)(2,1)S(1)}, bf16[128,576]{0,1:T(8,128)(2,1)}, u32[]{:S(2)}) copy-start(bf16[128,576]{0,1:T(8,128)(2,1)} %param.9) | copy-start | bytes 442372
  33.1 15.6 %copy-start.12 = (s32[1,2]{1,0:T(1,128)S(1)}, s32[1,2]{1,0:T(1,128)}, u32[]{:S(2)}) copy-start(s32[1,2]{1,0:T(1,128)} %param.15) | copy-start | bytes 28
  33.1 15.7 %copy-start.11 = (s32[128,1]{0,1:T(1,128)S(1)}, s32[128,1]{0,1:T(1,128)}, u32[]{:S(2)}) copy-start(s32[128,1]{0,1:T(1,128)} %param.12) | copy-start | bytes 1540
  33.1 44.3 %all-to-all-start.1 = ((bf16[8,128,1152]{2,1,0:T(8,128)(2,1)}), bf16[8,128,1152]{2,1,0:T(8,128)(2,1)}, u32[]{:S(2)}, u32[]{:S(2)}) async-start(bf16[8,128,1152]{2,1,0:T(8,128)(2,1)} %bitcast.12), calls=%async_computation.1 | async-start | bytes 4718592 | tf_op jit(solution)/shard_map/all_to_all | solution.py:292
  48.3 16.1 %copy-start.7 = (bf16[128,576]{1,0:T(8,128)(2,1)}, bf16[128,576]{1,0:T(8,128)(2,1)S(1)}, u32[]{:S(2)}) copy-start(bf16[128,576]{1,0:T(8,128)(2,1)S(1)} %copy.34.own_ref) | copy-start | bytes 442372
  49.5 10.8 %collective-permute-start.4 = (bf16[2,304,128]{2,1,0:T(8,128)(2,1)S(1)}, bf16[2,304,128]{2,1,0:T(8,128)(2,1)S(1)}, u32[]{:S(2)}, u32[]{:S(2)}) collective-permute-start(bf16[2,304,128]{2,1,0:T(8,128)(2,1)S(1)} %pad_maximum_fusion), channel_id=1, source_target_pairs={{0,2},{1,3},{2,0},{3,1},{4,6},{5,7},{6,4},{7,5},{8,10},{9,11},{10,... | collective-permute-start | bytes 466952 | tf_op jit(solution)/shard_map/ppermute | solution.py:305
  60.4 0.8 copy-start.3
  61.2 3.3 %copy-start.1 = (bf16[288,896]{1,0:T(8,128)(2,1)}, bf16[288,896]{1,0:T(8,128)(2,1)S(1)}, u32[]{:S(2)}) copy-start(bf16[288,896]{1,0:T(8,128)(2,1)S(1)} %get-tuple-element.52) | copy-start | bytes 1548292
  61.2 14.6 %collective-permute-start.5 = (bf16[288,896]{1,0:T(8,128)(2,1)S(1)}, bf16[288,896]{1,0:T(8,128)(2,1)S(1)}, u32[]{:S(2)}, u32[]{:S(2)}) collective-permute-start(bf16[288,896]{1,0:T(8,128)(2,1)S(1)} %get-tuple-element.46), channel_id=1, source_target_pairs={{0,192},{16,208},{32,224},{48,240},{64,128},{80,144},{96,160},{112... | collective-permute-start | bytes 1548296 | tf_op jit(solution)/shard_map/ppermute | solution.py:309
  62.5 19.8 %copy-start.10 = (f32[128,1]{0,1:T(1,128)S(1)}, f32[128,1]{0,1:T(1,128)}, u32[]{:S(2)}) copy-start(f32[128,1]{0,1:T(1,128)} %param.13) | copy-start | bytes 1540
  62.7 19.8 %copy-start.4 = (bf16[288,896]{1,0:T(8,128)(2,1)S(1)}, bf16[288,896]{1,0:T(8,128)(2,1)}, u32[]{:S(2)}) copy-start(bf16[288,896]{1,0:T(8,128)(2,1)} %copy-done.3) | copy-start | bytes 1548292
  75.7 0.8 copy-start.5
  76.5 17.3 %copy-start.2 = (bf16[288,896]{1,0:T(8,128)(2,1)S(1)}, bf16[288,896]{1,0:T(8,128)(2,1)}, u32[]{:S(2)}) copy-start(bf16[288,896]{1,0:T(8,128)(2,1)} %copy-done.1) | copy-start | bytes 1548292
  77.4 38.2 %all-to-all-start.2 = ((bf16[8,608,128]{2,1,0:T(8,128)(2,1)}), bf16[8,608,128]{2,1,0:T(8,128)(2,1)S(1)}, u32[]{:S(2)}, u32[]{:S(2)}) async-start(bf16[8,608,128]{2,1,0:T(8,128)(2,1)} %bitcast.15), calls=%async_computation.2 | async-start | bytes 2490368 | tf_op jit(solution)/shard_map/all_to_all | solution.py:292
  82.5 35.1 %collective-permute-start.6 = (bf16[288,896]{1,0:T(8,128)(2,1)S(1)}, bf16[288,896]{1,0:T(8,128)(2,1)}, u32[]{:S(2)}, u32[]{:S(2)}) collective-permute-start(bf16[288,896]{1,0:T(8,128)(2,1)S(1)} %copy-done.4), channel_id=1, source_target_pairs={{0,64},{16,80},{32,96},{48,112},{64,0},{80,16},{96,32},{112,48},{1... | collective-permute-start | bytes 1548296 | tf_op jit(solution)/shard_map/ppermute | solution.py:309
  93.8 23.7 %collective-permute-start.7 = (bf16[288,896]{1,0:T(8,128)(2,1)S(1)}, bf16[288,896]{1,0:T(8,128)(2,1)}, u32[]{:S(2)}, u32[]{:S(2)}) collective-permute-start(bf16[288,896]{1,0:T(8,128)(2,1)S(1)} %copy-done.2), channel_id=1, source_target_pairs={{0,128},{16,144},{32,160},{48,176},{64,192},{80,208},{96,224},{112... | collective-permute-start | bytes 1548296 | tf_op jit(solution)/shard_map/ppermute | solution.py:309
  117.6 1.0 copy-start.6

commit v3 on v2

--- a/solution.py
+++ b/solution.py
@@ -192,10 +192,10 @@
     row_refs, (out_ref, rows, sems) = refs[:-3], refs[-3:]
     tokens = slot_ref.shape[0]
     depth, part_width = rows.shape
-    share = row_refs[0].shape[0]
+    shares = [ref.shape[0] for ref in row_refs]
 
     def move(i):
-        return pltpu.make_async_copy(row_refs[i], rows.at[pl.ds(i * share, share)], sems.at[i])
+        return pltpu.make_async_copy(row_refs[i], rows.at[pl.ds(sum(shares[:i]), shares[i])], sems.at[i])
 
     for i in range(len(row_refs)):
         move(i).start()
@@ -301,12 +301,13 @@
     page_tiles = page_width // LANES
     tags = jnp.broadcast_to(page_table.reshape(new_count, 1, 1).astype(new_latent.dtype), (new_count, 16, LANES))
     tagged = jnp.concatenate([new_latent.reshape(new_count, page_tiles, LANES), tags], axis=1)
-    tagged, raw_far = lax.optimization_barrier((tagged, raw_far))
     tagged_far = lax.ppermute(tagged, "dp", across)
 
     met, tagged_far = lax.optimization_barrier((met, tagged_far))
     turned = turn(met)
-    arrived = [turned[0]] + [lax.ppermute(turned[k], "expert", along(k * side)) for k in range(1, side)]
+    early = turned[3].shape[0] * 3 // 4 // 16 * 16
+    arrived = [turned[0]] + [lax.ppermute(turned[k], "expert", along(k * side)) for k in range(1, side - 1)]
+    arrived += [lax.ppermute(half, "expert", along(3 * side)) for half in (turned[3][:early], turned[3][early:])]
 
     holders = listed // held_count
     rank = jnp.minimum(earlier_same(holders), PAIR - 1)

time: 126 us -> 135 us (1.071)
  waiting for transfers between devices: 19.9 us -> 41.9 us
  starting transfers between devices: 57.5 us -> 46.3 us
  local copies, waits for them, and re-layouts: 8.74 us -> 6.61 us
  other arithmetic: 2.54 us -> 4.14 us
    ppermute x3, waiting for transfers between devices: 0.01 us -> 29.2 us  [shards(): lax.ppermute(packed[far], 'expert', along(far))]
    ppermute x3 -> x2, waiting for transfers between devices: 11.3 us -> 3.15 us  [shards(): lax.ppermute(turned[k], 'expert', along(k * side))]
    all_to_all x2, starting transfers between devices: 20 us -> 12 us  [deliver(): lax.all_to_all(blocks, 'dp', 0, 0, axis_index_groups=halves, tiled=True)]
    ppermute x0 -> x2, waiting for transfers between devices: none -> 7.4 us  [shards(): lax.ppermute(half, 'expert', along(3 * side))]
    ppermute x3 -> x2, starting transfers between devices: 13.3 us -> 7.31 us  [shards(): lax.ppermute(turned[k], 'expert', along(k * side))]
    ppermute x1, waiting for transfers between devices: 4.1 us -> 0.53 us  [shards(): tagged_far = lax.ppermute(tagged, 'dp', across)]
    ppermute x0 -> x2, starting transfers between devices: none -> 2.77 us  [shards(): lax.ppermute(half, 'expert', along(3 * side))]
    unnamed x31 -> x24, local copies, waits for them, and re-layouts: 6.75 us -> 4.6 us
  transfers between devices with their start and end apart: 11 -> 12, of which waited for: 4 -> 7; matrix products, arithmetic and copies ran while one was open for 6% -> 6% of each run, Pallas kernels for 21% -> 20%
where the time goes in v3:
time: 135 us; the launch traced here: 134 us
  starting transfers between devices  46.3 us (34%)
  waiting for transfers between devices  41.9 us (31%)
  Pallas kernels  34.4 us (25%)
  local copies, waits for them, and re-layouts  6.61 us (5%)
  other arithmetic  4.14 us (3%)
    ppermute x3, waiting for transfers between devices, shards(): lax.ppermute(packed[far], 'expert', along(far))  29.2 us
    pallas_call x1, Pallas kernels, attend(): pl.pallas_call(functools.partial(attend_kernel, step_pairs, width, len(bl...  21.1 us
    all_to_all x2, starting transfers between devices, deliver(): lax.all_to_all(blocks, 'dp', 0, 0, axis_index_groups=halves, tiled=True)  12 us
    ppermute x1, starting transfers between devices, shards(): raw_far = lax.ppermute(raw, 'dp', across)  7.83 us
    ppermute x2, waiting for transfers between devices, shards(): lax.ppermute(half, 'expert', along(3 * side))  7.4 us
    ppermute x2, starting transfers between devices, shards(): lax.ppermute(turned[k], 'expert', along(k * side))  7.31 us
    ppermute x1, starting transfers between devices, shards(): tagged_far = lax.ppermute(tagged, 'dp', across)  6.13 us
    pallas_call x1, Pallas kernels, combine(): pl.pallas_call(functools.partial(combine_kernel, parts), out_shape=jax.Sh...  5.61 us
  transfers between devices with their start and end apart: 12, of which 7 were waited for; matrix products, arithmetic and copies ran while one was open for 6% of the time, Pallas kernels for 20%

profile of v3, /device:TPU:1, one launch (start us, length us, event | category | flops | bytes accessed | tf_op | source)
XLA Modules:
  0.0 134.4 jit_solution(17907570585755253109)
XLA Ops:
  0.6 7.8 %collective-permute-start = (bf16[8,36864]{1,0:T(8,128)(2,1)}, bf16[8,36864]{1,0:T(8,128)(2,1)}, u32[]{:S(2)}, u32[]{:S(2)}) collective-permute-start(bf16[8,36864]{1,0:T(8,128)(2,1)} %bitcast.39), channel_id=1, source_target_pairs={{0,2},{1,3},{2,0},{3,1},{4,6},{5,7},{6,4},{7,5},{8,10},{9,11},{10,... | collective-permute-start | bytes 1769480 | tf_op jit(solution)/shard_map/ppermute | solution.py:267
  8.5 1.6 %copy-done = bf16[1,1,16,9,7168]{4,2,3,1,0:T(8,128)(2,1)S(1)} copy-done((bf16[1,1,16,9,7168]{4,2,3,1,0:T(8,128)(2,1)S(1)}, bf16[1,1,16,9,7168]{4,2,3,1,0:T(8,128)(2,1)}, u32[]{:S(2)}) %copy-start) | copy-done | bytes 2064408
  10.0 3.3 %pack_rows.1 = (bf16[288,896]{1,0:T(8,128)(2,1)S(1)}, bf16[288,896]{1,0:T(8,128)(2,1)S(1)}, bf16[288,896]{1,0:T(8,128)(2,1)S(1)}, bf16[288,896]{1,0:T(8,128)(2,1)S(1)}) custom-call(s32[1]{0:T(128)} %bitcast.1.here_ref, bf16[144,7168]{1,0:T(8,128)(2,1)S(1)} %bitcast.38), custom_call_target="tpu_custom_call" | custom-call | flops 2378170368 | bytes 4128768 | tf_op jit(solution)/shard_map/pack_rows/pallas_call | solution.py:157
  13.3 0.6 broadcast_in_dim.42
  13.9 5.4 %all-to-all-start = ((s32[8,1,16]{2,1,0:T(1,128)}), s32[8,1,16]{2,1,0:T(1,128)S(1)}, u32[]{:S(2)}, u32[]{:S(2)}) async-start(s32[8,1,16]{2,1,0:T(1,128)} %broadcast_in_dim.42), calls=%async_computation | async-start | bytes 8192 | tf_op jit(solution)/shard_map/all_to_all | solution.py:279
  19.3 1.2 collective-permute-start.1
  21.5 1.1 copy.43
  22.6 1.6 %all-to-all-done = s32[8,1,16]{2,1,0:T(1,128)S(1)} async-done(((s32[8,1,16]{2,1,0:T(1,128)}), s32[8,1,16]{2,1,0:T(1,128)S(1)}, u32[]{:S(2)}, u32[]{:S(2)}) %all-to-all-start) | async-done | bytes 544 | tf_op jit(solution)/shard_map/all_to_all | solution.py:279
  25.1 7.6 %collective-permute-done.1.refs_1_ = bf16[288,896]{1,0:T(8,128)(2,1)S(1)} collective-permute-done((bf16[288,896]{1,0:T(8,128)(2,1)S(1)}, bf16[288,896]{1,0:T(8,128)(2,1)S(1)}, u32[]{:S(2)}, u32[]{:S(2)}) %collective-permute-start.1) | collective-permute-done | bytes 516128 | tf_op jit(solution)/shard_map/ppermute | solution.py:295
  32.7 1.1 copy.42
  33.9 2.1 %pick_pages.3 = bf16[32,32,1152]{2,1,0:T(8,128)(2,1)} custom-call(s32[32]{0:T(128)S(1)} %reshape.157.index_ref, bf16[8,32,1152]{2,1,0:T(8,128)(2,1)S(1)} %bitcast.36, bf16[8,32,1152]{2,1,0:T(8,128)(2,1)S(1)} %bitcast.37), custom_call_target="tpu_custom_call" | custom-call | tf_op jit(solution)/shard_map/pick_pages/pallas_call | solution.py:28
  36.0 6.2 %all-to-all-start.1 = ((bf16[8,128,1152]{2,1,0:T(8,128)(2,1)}), bf16[8,128,1152]{2,1,0:T(8,128)(2,1)}, u32[]{:S(2)}, u32[]{:S(2)}) async-start(bf16[8,128,1152]{2,1,0:T(8,128)(2,1)} %bitcast.12), calls=%async_computation.1 | async-start | bytes 4718592 | tf_op jit(solution)/shard_map/all_to_all | solution.py:292
  42.3 0.7 pad_maximum_fusion.1
  42.9 6.1 %collective-permute-start.4 = (bf16[2,304,128]{2,1,0:T(8,128)(2,1)}, bf16[2,304,128]{2,1,0:T(8,128)(2,1)}, u32[]{:S(2)}, u32[]{:S(2)}) collective-permute-start(bf16[2,304,128]{2,1,0:T(8,128)(2,1)} %pad_maximum_fusion.1), channel_id=1, source_target_pairs={{0,2},{1,3},{2,0},{3,1},{4,6},{5,7},{6,4},{7,5},{8,10},{9,11},{10,... | collective-permute-start | bytes 466952 | tf_op jit(solution)/shard_map/ppermute | solution.py:304
  49.1 2.7 %collective-permute-start.2 = (bf16[288,896]{1,0:T(8,128)(2,1)S(1)}, bf16[288,896]{1,0:T(8,128)(2,1)S(1)}, u32[]{:S(2)}, u32[]{:S(2)}) collective-permute-start(bf16[288,896]{1,0:T(8,128)(2,1)S(1)} %get-tuple-element.37), channel_id=1, source_target_pairs={{0,32},{16,48},{32,0},{48,16},{64,96},{80,112},{96,64},{112,80},{1... | collective-permute-start | bytes 1548296 | tf_op jit(solution)/shard_map/ppermute | solution.py:295
  51.8 0.9 collective-permute-start.3
  53.8 9.9 %collective-permute-done.2.refs_2_ = bf16[288,896]{1,0:T(8,128)(2,1)S(1)} collective-permute-done((bf16[288,896]{1,0:T(8,128)(2,1)S(1)}, bf16[288,896]{1,0:T(8,128)(2,1)S(1)}, u32[]{:S(2)}, u32[]{:S(2)}) %collective-permute-start.2) | collective-permute-done | bytes 516128 | tf_op jit(solution)/shard_map/ppermute | solution.py:295
  63.7 11.6 %collective-permute-done.3.refs_3_ = bf16[288,896]{1,0:T(8,128)(2,1)S(1)} collective-permute-done((bf16[288,896]{1,0:T(8,128)(2,1)S(1)}, bf16[288,896]{1,0:T(8,128)(2,1)S(1)}, u32[]{:S(2)}, u32[]{:S(2)}) %collective-permute-start.3) | collective-permute-done | bytes 516128 | tf_op jit(solution)/shard_map/ppermute | solution.py:295
  75.5 1.4 %collective-permute-start.5 = (bf16[208,896]{1,0:T(8,128)(2,1)S(1)}, bf16[208,896]{1,0:T(8,128)(2,1)S(1)}, u32[]{:S(2)}, u32[]{:S(2)}) collective-permute-start(bf16[208,896]{1,0:T(8,128)(2,1)S(1)} %slice.13), channel_id=1, source_target_pairs={{0,192},{16,208},{32,224},{48,240},{64,128},{80,144},{96,160},{112... | collective-permute-start | bytes 1118216 | tf_op jit(solution)/shard_map/ppermute | solution.py:310
  76.9 0.9 pad_maximum_fusion.refs_0_
  78.1 1.7 %pick_pages.4 = bf16[16,304,128]{2,1,0:T(8,128)(2,1)} custom-call(s32[16]{0:T(128)S(1)} %compare_select_fusion.1.index_ref, bf16[4,304,128]{2,1,0:T(8,128)(2,1)S(1)} %pad_maximum_fusion.refs_0_), custom_call_target="tpu_custom_call" | custom-call | tf_op jit(solution)/shard_map/pick_pages/pallas_call | solution.py:28
  79.8 7.4 %collective-permute-done.5.refs_3_ = bf16[208,896]{1,0:T(8,128)(2,1)S(1)} collective-permute-done((bf16[208,896]{1,0:T(8,128)(2,1)S(1)}, bf16[208,896]{1,0:T(8,128)(2,1)S(1)}, u32[]{:S(2)}, u32[]{:S(2)}) %collective-permute-start.5) | collective-permute-done | bytes 372768 | tf_op jit(solution)/shard_map/ppermute | solution.py:310
  87.2 5.8 %all-to-all-start.2 = ((bf16[8,608,128]{2,1,0:T(8,128)(2,1)}), bf16[8,608,128]{2,1,0:T(8,128)(2,1)S(1)}, u32[]{:S(2)}, u32[]{:S(2)}) async-start(bf16[8,608,128]{2,1,0:T(8,128)(2,1)} %bitcast.15), calls=%async_computation.2 | async-start | bytes 2490368 | tf_op jit(solution)/shard_map/all_to_all | solution.py:292
  93.1 0.5 minimum_add_fusion.place_ref
  93.7 1.4 %collective-permute-start.8 = (bf16[80,896]{1,0:T(8,128)(2,1)S(1)}, bf16[80,896]{1,0:T(8,128)(2,1)S(1)}, u32[]{:S(2)}, u32[]{:S(2)}) collective-permute-start(bf16[80,896]{1,0:T(8,128)(2,1)S(1)} %slice.15), channel_id=1, source_target_pairs={{0,192},{16,208},{32,224},{48,240},{64,128},{80,144},{96,160},{112... | collective-permute-start | bytes 430088 | tf_op jit(solution)/shard_map/ppermute | solution.py:310
  95.1 6.7 %collective-permute-start.6 = (bf16[288,896]{1,0:T(8,128)(2,1)}, bf16[288,896]{1,0:T(8,128)(2,1)}, u32[]{:S(2)}, u32[]{:S(2)}) collective-permute-start(bf16[288,896]{1,0:T(8,128)(2,1)} %copy-done.3), channel_id=1, source_target_pairs={{0,64},{16,80},{32,96},{48,112},{64,0},{80,16},{96,32},{112,48},{1... | collective-permute-start | bytes 1548296 | tf_op jit(solution)/shard_map/ppermute | solution.py:309
  101.8 0.6 collective-permute-start.7
  102.4 21.1 %attend.1 = bf16[128,16384]{1,0:T(8,128)(2,1)} custom-call(s32[16]{0:T(128)} %minimum_add_fusion.place_ref, bf16[128,18432]{1,0:T(8,128)(2,1)} %q_ref.1, bf16[128,576]{1,0:T(8,128)(2,1)} %copy-done.4, bf16[32,32,1152]{2,1,0:T(8,128)(2,1)} %bitcast.13.refs_0_), custom_call_target="tpu_custom_call" | custom-call | flops 10267656192 | bytes 8912896 | tf_op jit(solution)/shard_map/attend/pallas_call | solution.py:107
  124.1 0.6 pick_pages.5
  124.7 0.7 reshape.164
  125.5 3.1 %collective-permute-done.7.refs_2_ = bf16[288,896]{1,0:T(8,128)(2,1)} collective-permute-done((bf16[288,896]{1,0:T(8,128)(2,1)S(1)}, bf16[288,896]{1,0:T(8,128)(2,1)}, u32[]{:S(2)}, u32[]{:S(2)}) %collective-permute-start.7) | collective-permute-done | bytes 516128 | tf_op jit(solution)/shard_map/ppermute | solution.py:309
  128.6 5.6 %combine.1 = bf16[128,7168]{1,0:T(8,128)(2,1)} custom-call(s32[128,1]{1,0:T(8,128)S(1)} %copy.36.slot_ref, f32[128,1]{1,0:T(8,128)S(1)} %copy.37.gate_ref, bf16[288,896]{1,0:T(8,128)(2,1)S(1)} %get-tuple-element.48.refs_0_, bf16[288,896]{1,0:T(8,128)(2,1)} %collective-permute-done.6.refs_1_, bf16[288,896]{1,0:T(8,128)(2,1)} %collective-permute-done.7.refs_2_, ...), custom_call_target="tpu_custom_call" | custom-call | flops 2113929216 | bytes 3899392 | tf_op jit(solution)/shard_map/combine/pallas_call | solution.py:219
  (60 shorter events, 4.2 us)
Async XLA Ops:
  0.6 32.1 %collective-permute-start = (bf16[8,36864]{1,0:T(8,128)(2,1)}, bf16[8,36864]{1,0:T(8,128)(2,1)}, u32[]{:S(2)}, u32[]{:S(2)}) collective-permute-start(bf16[8,36864]{1,0:T(8,128)(2,1)} %bitcast.39), channel_id=1, source_target_pairs={{0,2},{1,3},{2,0},{3,1},{4,6},{5,7},{6,4},{7,5},{8,10},{9,11},{10,... | collective-permute-start | bytes 1769480 | tf_op jit(solution)/shard_map/ppermute | solution.py:267
  8.5 1.6 %copy-start = (bf16[1,1,16,9,7168]{4,2,3,1,0:T(8,128)(2,1)S(1)}, bf16[1,1,16,9,7168]{4,2,3,1,0:T(8,128)(2,1)}, u32[]{:S(2)}) copy-start(bf16[1,1,16,9,7168]{4,2,3,1,0:T(8,128)(2,1)} %param.14) | copy-start | bytes 6193156
  10.0 3.3 %copy-start.6 = (s32[1,16]{1,0:T(1,128)S(1)}, s32[1,16]{1,0:T(1,128)}, u32[]{:S(2)}) copy-start(s32[1,16]{1,0:T(1,128)} %param.11) | copy-start | bytes 196
  10.0 10.6 %copy-start.5 = (bf16[128,576]{0,1:T(8,128)(2,1)S(1)}, bf16[128,576]{0,1:T(8,128)(2,1)}, u32[]{:S(2)}) copy-start(bf16[128,576]{0,1:T(8,128)(2,1)} %param.9) | copy-start | bytes 442372
  13.9 10.3 %all-to-all-start = ((s32[8,1,16]{2,1,0:T(1,128)}), s32[8,1,16]{2,1,0:T(1,128)S(1)}, u32[]{:S(2)}, u32[]{:S(2)}) async-start(s32[8,1,16]{2,1,0:T(1,128)} %broadcast_in_dim.42), calls=%async_computation | async-start | bytes 8192 | tf_op jit(solution)/shard_map/all_to_all | solution.py:279
  19.3 13.4 %collective-permute-start.1 = (bf16[288,896]{1,0:T(8,128)(2,1)S(1)}, bf16[288,896]{1,0:T(8,128)(2,1)S(1)}, u32[]{:S(2)}, u32[]{:S(2)}) collective-permute-start(bf16[288,896]{1,0:T(8,128)(2,1)S(1)} %get-tuple-element.33), channel_id=1, source_target_pairs={{0,16},{16,0},{32,48},{48,32},{64,80},{80,64},{96,112},{112,96},{1... | collective-permute-start | bytes 1548296 | tf_op jit(solution)/shard_map/ppermute | solution.py:295
  20.8 0.7 copy-start.4
  36.0 6.2 %copy-start.9 = (s32[1,2]{1,0:T(1,128)S(1)}, s32[1,2]{1,0:T(1,128)}, u32[]{:S(2)}) copy-start(s32[1,2]{1,0:T(1,128)} %param.15) | copy-start | bytes 28
  36.0 16.7 %copy-start.8 = (s32[128,1]{0,1:T(1,128)S(1)}, s32[128,1]{0,1:T(1,128)}, u32[]{:S(2)}) copy-start(s32[128,1]{0,1:T(1,128)} %param.12) | copy-start | bytes 1540
  36.0 51.2 %all-to-all-start.1 = ((bf16[8,128,1152]{2,1,0:T(8,128)(2,1)}), bf16[8,128,1152]{2,1,0:T(8,128)(2,1)}, u32[]{:S(2)}, u32[]{:S(2)}) async-start(bf16[8,128,1152]{2,1,0:T(8,128)(2,1)} %bitcast.12), calls=%async_computation.1 | async-start | bytes 4718592 | tf_op jit(solution)/shard_map/all_to_all | solution.py:292
  42.9 10.8 %collective-permute-start.4 = (bf16[2,304,128]{2,1,0:T(8,128)(2,1)}, bf16[2,304,128]{2,1,0:T(8,128)(2,1)}, u32[]{:S(2)}, u32[]{:S(2)}) collective-permute-start(bf16[2,304,128]{2,1,0:T(8,128)(2,1)} %pad_maximum_fusion.1), channel_id=1, source_target_pairs={{0,2},{1,3},{2,0},{3,1},{4,6},{5,7},{6,4},{7,5},{8,10},{9,11},{10,... | collective-permute-start | bytes 466952 | tf_op jit(solution)/shard_map/ppermute | solution.py:304
  49.1 14.6 %collective-permute-start.2 = (bf16[288,896]{1,0:T(8,128)(2,1)S(1)}, bf16[288,896]{1,0:T(8,128)(2,1)S(1)}, u32[]{:S(2)}, u32[]{:S(2)}) collective-permute-start(bf16[288,896]{1,0:T(8,128)(2,1)S(1)} %get-tuple-element.37), channel_id=1, source_target_pairs={{0,32},{16,48},{32,0},{48,16},{64,96},{80,112},{96,64},{112,80},{1... | collective-permute-start | bytes 1548296 | tf_op jit(solution)/shard_map/ppermute | solution.py:295
  51.8 23.5 %collective-permute-start.3 = (bf16[288,896]{1,0:T(8,128)(2,1)S(1)}, bf16[288,896]{1,0:T(8,128)(2,1)S(1)}, u32[]{:S(2)}, u32[]{:S(2)}) collective-permute-start(bf16[288,896]{1,0:T(8,128)(2,1)S(1)} %get-tuple-element.38), channel_id=1, source_target_pairs={{0,48},{16,32},{32,16},{48,0},{64,112},{80,96},{96,80},{112,64},{1... | collective-permute-start | bytes 1548296 | tf_op jit(solution)/shard_map/ppermute | solution.py:295
  75.5 2.6 %copy-start.1 = (bf16[288,896]{1,0:T(8,128)(2,1)}, bf16[288,896]{1,0:T(8,128)(2,1)S(1)}, u32[]{:S(2)}) copy-start(bf16[288,896]{1,0:T(8,128)(2,1)S(1)} %get-tuple-element.50) | copy-start | bytes 1548292
  75.5 2.6 %copy-start.3 = (bf16[288,896]{1,0:T(8,128)(2,1)}, bf16[288,896]{1,0:T(8,128)(2,1)S(1)}, u32[]{:S(2)}) copy-start(bf16[288,896]{1,0:T(8,128)(2,1)S(1)} %get-tuple-element.49) | copy-start | bytes 1548292
  75.5 11.7 %collective-permute-start.5 = (bf16[208,896]{1,0:T(8,128)(2,1)S(1)}, bf16[208,896]{1,0:T(8,128)(2,1)S(1)}, u32[]{:S(2)}, u32[]{:S(2)}) collective-permute-start(bf16[208,896]{1,0:T(8,128)(2,1)S(1)} %slice.13), channel_id=1, source_target_pairs={{0,192},{16,208},{32,224},{48,240},{64,128},{80,144},{96,160},{112... | collective-permute-start | bytes 1118216 | tf_op jit(solution)/shard_map/ppermute | solution.py:310
  77.8 15.7 %copy-start.7 = (f32[128,1]{0,1:T(1,128)S(1)}, f32[128,1]{0,1:T(1,128)}, u32[]{:S(2)}) copy-start(f32[128,1]{0,1:T(1,128)} %param.13) | copy-start | bytes 1540
  78.1 23.7 %copy-start.2 = (bf16[288,896]{1,0:T(8,128)(2,1)S(1)}, bf16[288,896]{1,0:T(8,128)(2,1)}, u32[]{:S(2)}) copy-start(bf16[288,896]{1,0:T(8,128)(2,1)} %copy-done.1) | copy-start | bytes 1548292
  87.2 36.3 %all-to-all-start.2 = ((bf16[8,608,128]{2,1,0:T(8,128)(2,1)}), bf16[8,608,128]{2,1,0:T(8,128)(2,1)S(1)}, u32[]{:S(2)}, u32[]{:S(2)}) async-start(bf16[8,608,128]{2,1,0:T(8,128)(2,1)} %bitcast.15), calls=%async_computation.2 | async-start | bytes 2490368 | tf_op jit(solution)/shard_map/all_to_all | solution.py:292
  93.7 31.7 %collective-permute-start.8 = (bf16[80,896]{1,0:T(8,128)(2,1)S(1)}, bf16[80,896]{1,0:T(8,128)(2,1)S(1)}, u32[]{:S(2)}, u32[]{:S(2)}) collective-permute-start(bf16[80,896]{1,0:T(8,128)(2,1)S(1)} %slice.15), channel_id=1, source_target_pairs={{0,192},{16,208},{32,224},{48,240},{64,128},{80,144},{96,160},{112... | collective-permute-start | bytes 430088 | tf_op jit(solution)/shard_map/ppermute | solution.py:310
  95.1 30.4 %collective-permute-start.6 = (bf16[288,896]{1,0:T(8,128)(2,1)}, bf16[288,896]{1,0:T(8,128)(2,1)}, u32[]{:S(2)}, u32[]{:S(2)}) collective-permute-start(bf16[288,896]{1,0:T(8,128)(2,1)} %copy-done.3), channel_id=1, source_target_pairs={{0,64},{16,80},{32,96},{48,112},{64,0},{80,16},{96,32},{112,48},{1... | collective-permute-start | bytes 1548296 | tf_op jit(solution)/shard_map/ppermute | solution.py:309
  101.8 26.8 %collective-permute-start.7 = (bf16[288,896]{1,0:T(8,128)(2,1)S(1)}, bf16[288,896]{1,0:T(8,128)(2,1)}, u32[]{:S(2)}, u32[]{:S(2)}) collective-permute-start(bf16[288,896]{1,0:T(8,128)(2,1)S(1)} %copy-done.2), channel_id=1, source_target_pairs={{0,128},{16,144},{32,160},{48,176},{64,192},{80,208},{96,224},{112... | collective-permute-start | bytes 1548296 | tf_op jit(solution)/shard_map/ppermute | solution.py:309
